TPU v7x, 32 devices: a whole 2x2x4 slice. The times are simulated.
32 devices in a mesh: lat: 4 (over z), lon: 8 (over y, x, core).
Axes of the slice: x: 2, y: 2, z: 4, core: 2. Of those that a mesh axis runs over, the one named last changes fastest.
Arguments:
- fields: float32 [256, 256, 256], P('lat', 'lon'), may hold values from -6 to 6
- land_sea: int32 [128, 128], P('lat', 'lon'), may hold values 0 or 1
- w_depth: float32 [3, 3, 256], replicated, may hold values from -2 to 2
- b_depth: float32 [256], replicated, may hold values from -3 to 3
- w_one: bfloat16 [3, 3, 256, 300], replicated, may hold values from -0.125 to 0.125
- b_one: float32 [300], replicated, may hold values from -3 to 3
- w_two: bfloat16 [3, 3, 300, 300], replicated, may hold values from -0.125 to 0.125
- b_two: float32 [300], replicated, may hold values from -3 to 3
Outputs:
- level_out: float32 [128, 128, 300], P('lat', 'lon')
All inputs are finite; a program needn't handle non-finite values. No bound on the sum of `land_sea` on one device may be relied on, other than what follows from the above.
Results may differ from a plain program's by a relative error of at most 0.0035.
Values may be sent and summed in bfloat16 or wider, within the bound.
A program may use at most 64 MiB of HBM per device.

v0:
```python
import jax
import jax.numpy as jnp
from jax import lax
from jax.sharding import PartitionSpec as P


def shifted(block, axis, distance):
    devices = range(lax.axis_size(axis))
    route = [(i - distance, i) for i in devices if i - distance in devices]
    return lax.ppermute(block, axis, route)


def from_behind(array, axis, by):
    devices = lax.axis_size(axis)
    return lax.ppermute(array, axis, [(i, (i + by) % devices) for i in range(devices)])


def padded(cells, sides, width):
    for axis, dim in sides:
        count = lax.axis_size(axis)
        head = lax.slice_in_dim(cells, 0, width, axis=dim)
        tail = lax.slice_in_dim(cells, cells.shape[dim] - width, cells.shape[dim], axis=dim)
        cells = jnp.concatenate(
            [
                lax.ppermute(tail, axis, [(i, (i + 1) % count) for i in range(count)]),
                cells,
                lax.ppermute(head, axis, [((i + 1) % count, i) for i in range(count)]),
            ],
            axis=dim,
        )
    return cells


def clear_poles(ext, width, band_rows):
    total_rows = lax.axis_size("lat") * band_rows
    row_index = (
        lax.axis_index("lat") * band_rows + jnp.arange(ext.shape[0], dtype=jnp.int32) - width
    )
    keeping = (row_index >= 0) & (row_index < total_rows)
    return jnp.where(keeping[:, None, None], ext, jnp.zeros_like(ext))


def dilated(ext, kernel, bias, reach, rows, cols):
    out_ch = kernel.shape[3]
    total = jnp.zeros((rows, cols, out_ch), jnp.float32) + bias
    for a in range(3):
        band = ext[a * reach : a * reach + rows]
        taps = jnp.concatenate([kernel[a, 0], kernel[a, 1], kernel[a, 2]], axis=1)
        product = jnp.einsum("ijc,cd->ijd", band, taps, preferred_element_type=jnp.float32)
        for b in range(3):
            total = total + product[:, b * reach : b * reach + cols, b * out_ch : (b + 1) * out_ch]
    return total


def on_device(fields, land_sea, w_depth, b_depth, w_one, b_one, w_two, b_two):
    rows = land_sea.shape[0]
    cols = land_sea.shape[1]
    chans = fields.shape[2]
    north = shifted(fields[-1:], "lat", 1)
    edge_column = jnp.concatenate([north[:, -1:], fields[:, -1:]], axis=0)
    west = from_behind(edge_column, "lon", 1)
    phases = fields.reshape(rows, 2, cols, 2, chans)
    rows_even = phases[:, 0]
    rows_odd = phases[:, 1]
    rows_prev = jnp.concatenate([north.reshape(1, cols, 2, chans), rows_odd[:-1]], axis=0)
    row_sets = (rows_prev, rows_even, rows_odd)
    west_sets = (west[0 : 2 * rows : 2], west[1 : 2 * rows + 1 : 2], west[2 : 2 * rows + 1 : 2])
    down = jnp.zeros((rows, cols, chans), jnp.float32) + b_depth
    for a in range(3):
        chosen = row_sets[a]
        col_prev = jnp.concatenate([west_sets[a], chosen[:, :-1, 1]], axis=1)
        down = (
            down
            + col_prev * w_depth[a, 0]
            + chosen[:, :, 0] * w_depth[a, 1]
            + chosen[:, :, 1] * w_depth[a, 2]
        )
    mask = land_sea.astype(jnp.float32)[:, :, None]
    down_bf = (down * mask).astype(jnp.bfloat16)
    framed = padded(down_bf, (("lat", 0), ("lon", 1)), 4)
    framed = clear_poles(framed, 4, rows)
    hidden = jax.nn.gelu(dilated(framed, w_one, b_one, 4, rows, cols), approximate=False).astype(
        jnp.bfloat16
    )
    outer = padded(hidden, (("lat", 0), ("lon", 1)), 8)
    outer = clear_poles(outer, 8, rows)
    return jax.nn.gelu(dilated(outer, w_two, b_two, 8, rows, cols), approximate=False) * mask


def solution(mesh):
    return jax.shard_map(
        on_device,
        mesh=mesh,
        in_specs=(P("lat", "lon", None), P("lat", "lon"), P(), P(), P(), P(), P(), P()),
        out_specs=P("lat", "lon", None),
        check_vma=False,
    )
```

profile of v0, /device:TPU:0, one launch (start us, length us, event | category | flops | bytes accessed | tf_op | source)
XLA Modules:
  0.0 62.8 jit_solution(14528959860246554152)
XLA Ops:
  0.8 4.9 %collective-permute-start = (f32[1,32,256]{2,1,0:T(8,128)S(1)}, f32[1,32,256]{2,1,0:T(8,128)S(1)}, u32[]{:S(2)}, u32[]{:S(2)}) collective-permute-start(f32[1,32,256]{2,1,0:T(8,128)S(1)} %slice.235), channel_id=1, source_target_pairs={{0,8},{8,16},{16,24},{1,9},{9,17},{17,25},{2,10},{10,18},{18,26},{... | collective-permute-start | bytes 98312 | tf_op jit(solution)/shard_map/ppermute | solution.py:10
  5.7 2.5 %reshape.28 = f32[32,2,16,2,256]{4,3,2,1,0:T(2,128)S(1)} reshape(f32[64,32,256]{2,1,0:T(8,128)} %param.8) | data formatting | bytes 4194304 | tf_op jit(solution)/shard_map/reshape | solution.py:62
  9.2 0.9 %slice_bitcast_fusion.2 = f32[32,15,256]{2,1,0:T(8,128)} fusion(f32[32,16,2,256]{3,1,0,2:T(8,128)S(1)} %get-tuple-element.45), kind=kLoop, calls=%fused_computation.101 | loop fusion | bytes 983040 | tf_op jit(solution)/shard_map/squeeze | solution.py:71
  11.4 1.1 %slice.237 = f32[64,1,256]{2,1,0:T(1,128)S(1)} slice(f32[64,32,256]{2,1,0:T(8,128)} %param.8), slice={[0:64], [31:32], [0:256]} | slice | bytes 131072 | tf_op jit(solution)/shard_map/slice | solution.py:60
  12.5 1.3 %slice.314 = f32[31,1,16,2,256]{4,3,2,1,0:T(2,128)} slice(f32[32,2,16,2,256]{4,3,2,1,0:T(2,128)S(1)} %reshape.28), slice={[0:31], [1:2], [0:16], [0:2], [0:256]} | slice | bytes 2031616 | tf_op jit(solution)/shard_map/slice | solution.py:65
  13.9 1.4 %copy.24 = f32[31,1,16,2,256]{4,2,0,3,1:T(8,128)S(1)} copy(f32[31,1,16,2,256]{4,3,2,1,0:T(2,128)} %slice.314) | data formatting | bytes 2031616
  15.6 4.5 %collective-permute-done.1 = f32[65,1,256]{2,1,0:T(1,128)S(1)} collective-permute-done((f32[65,1,256]{2,1,0:T(1,128)S(1)}, f32[65,1,256]{2,1,0:T(1,128)S(1)}, u32[]{:S(2)}, u32[]{:S(2)}) %collective-permute-start.1) | collective-permute-done | bytes 66592 | tf_op jit(solution)/shard_map/ppermute | solution.py:15
  20.2 1.4 %fusion.56 = bf16[32,16,256]{2,1,0:T(8,128)(2,1)S(1)} fusion(f32[32,16,2,256]{3,1,0,2:T(8,128)S(1)} %get-tuple-element.45, f32[32,15,256]{2,1,0:T(8,128)S(1)} %copy-done.3, f32[32,1,256]{2,1,0:T(1,128)S(1)} %get-tuple-element.34, f32[32,16,2,256]{3,1,0,2:T(8,128)S(1)} %copy-done.1, f32[32,15,256]{2,1,0:T(8,128)S(1)} %copy-done.4, ...), kind=kLoop, calls=%fused_computation.114 | loop fusion | flops 3276800 | bytes 4993024 | tf_op jit(solution)/shard_map/convert_element_type | solution.py:79
  21.6 1.6 %collective-permute-start.2 = (bf16[4,16,256]{2,1,0:T(8,128)(2,1)S(1)}, bf16[4,16,256]{2,1,0:T(8,128)(2,1)S(1)}, u32[]{:S(2)}, u32[]{:S(2)}) collective-permute-start(bf16[4,16,256]{2,1,0:T(8,128)(2,1)S(1)} %get-tuple-element.31), channel_id=1, source_target_pairs={{0,8},{8,16},{16,24},{24,0},{1,9},{9,17},{17,25},{25,1},{2,10},{10... | collective-permute-start | bytes 98312 | tf_op jit(solution)/shard_map/ppermute | solution.py:25
  23.3 2.2 %collective-permute-start.3 = (bf16[4,16,256]{2,1,0:T(8,128)(2,1)S(1)}, bf16[4,16,256]{2,1,0:T(8,128)(2,1)S(1)}, u32[]{:S(2)}, u32[]{:S(2)}) collective-permute-start(bf16[4,16,256]{2,1,0:T(8,128)(2,1)S(1)} %get-tuple-element.32), channel_id=1, source_target_pairs={{8,0},{16,8},{24,16},{0,24},{9,1},{17,9},{25,17},{1,25},{10,2},{18... | collective-permute-start | bytes 98312 | tf_op jit(solution)/shard_map/ppermute | solution.py:27
  25.6 1.9 %collective-permute-done.2 = bf16[4,16,256]{2,1,0:T(8,128)(2,1)S(1)} collective-permute-done((bf16[4,16,256]{2,1,0:T(8,128)(2,1)S(1)}, bf16[4,16,256]{2,1,0:T(8,128)(2,1)S(1)}, u32[]{:S(2)}, u32[]{:S(2)}) %collective-permute-start.2) | collective-permute-done | bytes 32800 | tf_op jit(solution)/shard_map/ppermute | solution.py:25
  27.7 2.6 %collective-permute-start.5 = (bf16[40,4,256]{2,1,0:T(4,128)(2,1)S(1)}, bf16[40,4,256]{2,1,0:T(4,128)(2,1)S(1)}, u32[]{:S(2)}, u32[]{:S(2)}) collective-permute-start(bf16[40,4,256]{2,1,0:T(4,128)(2,1)S(1)} %get-tuple-element.30), channel_id=1, source_target_pairs={{1,0},{2,1},{3,2},{4,3},{5,4},{6,5},{7,6},{0,7},{9,8},{10,9},{11,1... | collective-permute-start | bytes 245768 | tf_op jit(solution)/shard_map/ppermute | solution.py:27
  30.3 2.1 %collective-permute-done.4 = bf16[40,4,256]{2,1,0:T(4,128)(2,1)S(1)} collective-permute-done((bf16[40,4,256]{2,1,0:T(4,128)(2,1)S(1)}, bf16[40,4,256]{2,1,0:T(4,128)(2,1)S(1)}, u32[]{:S(2)}, u32[]{:S(2)}) %collective-permute-start.4) | collective-permute-done | bytes 81952 | tf_op jit(solution)/shard_map/ppermute | solution.py:25
  34.4 2.7 %fusion.2 = bf16[32,16,300]{2,1,0:T(8,128)(2,1)S(1)} fusion(f32[32,24,900]{2,1,0:T(8,128)S(1)} %fusion.67, f32[32,24,900]{2,1,0:T(8,128)S(1)} %fusion.62, f32[32,24,900]{2,1,0:T(8,128)S(1)} %fusion.57, f32[300]{0:T(512)S(1)} %copy-done.9), kind=kLoop, calls=%fused_computation.12 | loop fusion | flops 11366400 | bytes 5838000 | tf_op jit(solution)/shard_map/convert_element_type | solution.py:82
  37.1 1.3 %collective-permute-start.6 = (bf16[8,16,300]{2,1,0:T(8,128)(2,1)S(1)}, bf16[8,16,300]{2,1,0:T(8,128)(2,1)S(1)}, u32[]{:S(2)}, u32[]{:S(2)}) collective-permute-start(bf16[8,16,300]{2,1,0:T(8,128)(2,1)S(1)} %get-tuple-element.27), channel_id=1, source_target_pairs={{0,8},{8,16},{16,24},{24,0},{1,9},{9,17},{17,25},{25,1},{2,10},{10... | collective-permute-start | bytes 230408 | tf_op jit(solution)/shard_map/ppermute | solution.py:25
  38.4 2.6 %collective-permute-start.7 = (bf16[8,16,300]{2,1,0:T(8,128)(2,1)S(1)}, bf16[8,16,300]{2,1,0:T(8,128)(2,1)S(1)}, u32[]{:S(2)}, u32[]{:S(2)}) collective-permute-start(bf16[8,16,300]{2,1,0:T(8,128)(2,1)S(1)} %get-tuple-element.28), channel_id=1, source_target_pairs={{8,0},{16,8},{24,16},{0,24},{9,1},{17,9},{25,17},{1,25},{10,2},{18... | collective-permute-start | bytes 230408 | tf_op jit(solution)/shard_map/ppermute | solution.py:27
  41.0 3.7 %collective-permute-done.6 = bf16[8,16,300]{2,1,0:T(8,128)(2,1)S(1)} collective-permute-done((bf16[8,16,300]{2,1,0:T(8,128)(2,1)S(1)}, bf16[8,16,300]{2,1,0:T(8,128)(2,1)S(1)}, u32[]{:S(2)}, u32[]{:S(2)}) %collective-permute-start.6) | collective-permute-done | bytes 76832 | tf_op jit(solution)/shard_map/ppermute | solution.py:25
  44.6 0.9 %collective-permute-done.7 = bf16[8,16,300]{2,1,0:T(8,128)(2,1)S(1)} collective-permute-done((bf16[8,16,300]{2,1,0:T(8,128)(2,1)S(1)}, bf16[8,16,300]{2,1,0:T(8,128)(2,1)S(1)}, u32[]{:S(2)}, u32[]{:S(2)}) %collective-permute-start.7) | collective-permute-done | bytes 76832 | tf_op jit(solution)/shard_map/ppermute | solution.py:27
  45.8 2.6 %collective-permute-start.9 = (bf16[48,8,300]{2,1,0:T(8,128)(2,1)S(1)}, bf16[48,8,300]{2,1,0:T(8,128)(2,1)S(1)}, u32[]{:S(2)}, u32[]{:S(2)}) collective-permute-start(bf16[48,8,300]{2,1,0:T(8,128)(2,1)S(1)} %get-tuple-element.26), channel_id=1, source_target_pairs={{1,0},{2,1},{3,2},{4,3},{5,4},{6,5},{7,6},{0,7},{9,8},{10,9},{11,1... | collective-permute-start | bytes 691208 | tf_op jit(solution)/shard_map/ppermute | solution.py:27
  48.6 6.9 %collective-permute-done.8 = bf16[48,8,300]{2,1,0:T(8,128)(2,1)S(1)} collective-permute-done((bf16[48,8,300]{2,1,0:T(8,128)(2,1)S(1)}, bf16[48,8,300]{2,1,0:T(8,128)(2,1)S(1)}, u32[]{:S(2)}, u32[]{:S(2)}) %collective-permute-start.8) | collective-permute-done | bytes 230432 | tf_op jit(solution)/shard_map/ppermute | solution.py:25
  55.6 1.3 %fusion.25 = f32[32,32,900]{2,1,0:T(8,128)S(1)} fusion(bf16[300,300]{1,0:T(8,128)(2,1)S(1)} %get-tuple-element.7, bf16[300,300]{1,0:T(8,128)(2,1)S(1)} %get-tuple-element.8, bf16[300,300]{1,0:T(8,128)(2,1)S(1)} %get-tuple-element.9, bf16[48,8,300]{2,1,0:T(8,128)(2,1)S(1)} %collective-permute-done.9, bf16[8,16,300]{2,1,0:T(8,128)(2,1)S(1)} %collective-permute-done.7, ...), kind=kOutput, calls=%fused_computation.71 | convolution fusion | flops 559648768 | bytes 5148048 | tf_op jit(solution)/shard_map/ijc,cd->ijd/dot_general | solution.py:49
  56.9 1.3 %fusion.30 = f32[32,32,900]{2,1,0:T(8,128)S(1)} fusion(bf16[300,300]{1,0:T(8,128)(2,1)S(1)} %get-tuple-element.12, bf16[300,300]{1,0:T(8,128)(2,1)S(1)} %get-tuple-element.13, bf16[300,300]{1,0:T(8,128)(2,1)S(1)} %get-tuple-element.6, bf16[48,8,300]{2,1,0:T(8,128)(2,1)S(1)} %collective-permute-done.9, bf16[8,16,300]{2,1,0:T(8,128)(2,1)S(1)} %collective-permute-done.7, ...), kind=kOutput, calls=%fused_computation.77 | convolution fusion | flops 559648768 | bytes 5148048 | tf_op jit(solution)/shard_map/ijc,cd->ijd/dot_general | solution.py:49
  58.3 1.3 %fusion.20 = f32[32,32,900]{2,1,0:T(8,128)S(1)} fusion(bf16[300,300]{1,0:T(8,128)(2,1)S(1)} %get-tuple-element.10, bf16[300,300]{1,0:T(8,128)(2,1)S(1)} %get-tuple-element.11, bf16[300,300]{1,0:T(8,128)(2,1)S(1)} %get-tuple-element.5, bf16[48,8,300]{2,1,0:T(8,128)(2,1)S(1)} %collective-permute-done.9, bf16[8,16,300]{2,1,0:T(8,128)(2,1)S(1)} %collective-permute-done.7, ...), kind=kOutput, calls=%fused_computation.65 | convolution fusion | flops 559648768 | bytes 5148048 | tf_op jit(solution)/shard_map/ijc,cd->ijd/dot_general | solution.py:49
  59.6 3.1 %fusion.5 = f32[32,16,300]{2,1,0:T(8,128)} fusion(f32[32,32,900]{2,1,0:T(8,128)S(1)} %fusion.30, f32[32,32,900]{2,1,0:T(8,128)S(1)} %fusion.25, f32[32,32,900]{2,1,0:T(8,128)S(1)} %fusion.20, f32[32,16]{1,0:T(8,128)S(1)} %copy.16, f32[300]{0:T(512)S(1)} %copy-done.8), kind=kLoop, calls=%fused_computation.15 | loop fusion | flops 11366400 | bytes 6147248 | tf_op jit(solution)/shard_map/mul | solution.py:87
  (52 shorter events, 6.1 us)
Async XLA Ops:
  0.8 14.6 %collective-permute-start = (f32[1,32,256]{2,1,0:T(8,128)S(1)}, f32[1,32,256]{2,1,0:T(8,128)S(1)}, u32[]{:S(2)}, u32[]{:S(2)}) collective-permute-start(f32[1,32,256]{2,1,0:T(8,128)S(1)} %slice.235), channel_id=1, source_target_pairs={{0,8},{8,16},{16,24},{1,9},{9,17},{17,25},{2,10},{10,18},{18,26},{... | collective-permute-start | bytes 98312 | tf_op jit(solution)/shard_map/ppermute | solution.py:10
  8.9 2.0 %copy-start.7 = (f32[3,3,256]{2,1,0:T(4,128)S(1)}, f32[3,3,256]{2,1,0:T(4,128)}, u32[]{:S(2)}) copy-start(f32[3,3,256]{2,1,0:T(4,128)} %param.10) | copy-start | bytes 27652
  9.1 4.7 %copy-start = (f32[32,16,2,256]{3,1,0,2:T(8,128)}, f32[32,16,2,256]{3,1,0,2:T(8,128)S(1)}, u32[]{:S(2)}) copy-start(f32[32,16,2,256]{3,1,0,2:T(8,128)S(1)} %get-tuple-element.46) | copy-start | bytes 3145732
  9.1 4.7 %copy-start.6 = (s32[32,16]{0,1:T(8,128)S(1)}, s32[32,16]{0,1:T(8,128)}, u32[]{:S(2)}) copy-start(s32[32,16]{0,1:T(8,128)} %param.9) | copy-start | bytes 6148
  13.8 6.4 %copy-start.3 = (f32[32,15,256]{2,1,0:T(8,128)S(1)}, f32[32,15,256]{2,1,0:T(8,128)}, u32[]{:S(2)}) copy-start(f32[32,15,256]{2,1,0:T(8,128)} %slice_bitcast_fusion.2) | copy-start | bytes 1474564
  13.8 6.4 %copy-start.4 = (f32[32,15,256]{2,1,0:T(8,128)S(1)}, f32[32,15,256]{2,1,0:T(8,128)}, u32[]{:S(2)}) copy-start(f32[32,15,256]{2,1,0:T(8,128)} %slice_bitcast_fusion.5) | copy-start | bytes 1474564
  15.4 4.8 %copy-start.1 = (f32[32,16,2,256]{3,1,0,2:T(8,128)S(1)}, f32[32,16,2,256]{3,1,0,2:T(8,128)}, u32[]{:S(2)}) copy-start(f32[32,16,2,256]{3,1,0,2:T(8,128)} %copy-done) | copy-start | bytes 3145732
  15.5 4.7 %collective-permute-start.1 = (f32[65,1,256]{2,1,0:T(1,128)S(1)}, f32[65,1,256]{2,1,0:T(1,128)S(1)}, u32[]{:S(2)}, u32[]{:S(2)}) collective-permute-start(f32[65,1,256]{2,1,0:T(1,128)S(1)} %pad_maximum_fusion.5), channel_id=1, source_target_pairs={{0,1},{1,2},{2,3},{3,4},{4,5},{5,6},{6,7},{7,0},{8,9},{9,10},{10,1... | collective-permute-start | bytes 199688 | tf_op jit(solution)/shard_map/ppermute | solution.py:15
  20.2 5.3 %copy-start.5 = (bf16[3,3,256,300]{2,3,1,0:T(8,128)(2,1)S(1)}, bf16[3,3,256,300]{2,3,1,0:T(8,128)(2,1)}, u32[]{:S(2)}) copy-start(bf16[3,3,256,300]{2,3,1,0:T(8,128)(2,1)} %param.12) | copy-start | bytes 4147204
  21.6 5.9 %collective-permute-start.2 = (bf16[4,16,256]{2,1,0:T(8,128)(2,1)S(1)}, bf16[4,16,256]{2,1,0:T(8,128)(2,1)S(1)}, u32[]{:S(2)}, u32[]{:S(2)}) collective-permute-start(bf16[4,16,256]{2,1,0:T(8,128)(2,1)S(1)} %get-tuple-element.31), channel_id=1, source_target_pairs={{0,8},{8,16},{16,24},{24,0},{1,9},{9,17},{17,25},{25,1},{2,10},{10... | collective-permute-start | bytes 98312 | tf_op jit(solution)/shard_map/ppermute | solution.py:25
  23.3 4.3 %collective-permute-start.3 = (bf16[4,16,256]{2,1,0:T(8,128)(2,1)S(1)}, bf16[4,16,256]{2,1,0:T(8,128)(2,1)S(1)}, u32[]{:S(2)}, u32[]{:S(2)}) collective-permute-start(bf16[4,16,256]{2,1,0:T(8,128)(2,1)S(1)} %get-tuple-element.32), channel_id=1, source_target_pairs={{8,0},{16,8},{24,16},{0,24},{9,1},{17,9},{25,17},{1,25},{10,2},{18... | collective-permute-start | bytes 98312 | tf_op jit(solution)/shard_map/ppermute | solution.py:27
  27.6 4.8 %collective-permute-start.4 = (bf16[40,4,256]{2,1,0:T(4,128)(2,1)S(1)}, bf16[40,4,256]{2,1,0:T(4,128)(2,1)S(1)}, u32[]{:S(2)}, u32[]{:S(2)}) collective-permute-start(bf16[40,4,256]{2,1,0:T(4,128)(2,1)S(1)} %get-tuple-element.29), channel_id=1, source_target_pairs={{0,1},{1,2},{2,3},{3,4},{4,5},{5,6},{6,7},{7,0},{8,9},{9,10},{10,1... | collective-permute-start | bytes 245768 | tf_op jit(solution)/shard_map/ppermute | solution.py:25
  27.7 4.8 %collective-permute-start.5 = (bf16[40,4,256]{2,1,0:T(4,128)(2,1)S(1)}, bf16[40,4,256]{2,1,0:T(4,128)(2,1)S(1)}, u32[]{:S(2)}, u32[]{:S(2)}) collective-permute-start(bf16[40,4,256]{2,1,0:T(4,128)(2,1)S(1)} %get-tuple-element.30), channel_id=1, source_target_pairs={{1,0},{2,1},{3,2},{4,3},{5,4},{6,5},{7,6},{0,7},{9,8},{10,9},{11,1... | collective-permute-start | bytes 245768 | tf_op jit(solution)/shard_map/ppermute | solution.py:27
  33.7 0.7 %copy-start.9 = (f32[300]{0:T(512)S(1)}, f32[300]{0:T(512)}, u32[]{:S(2)}) copy-start(f32[300]{0:T(512)} %param.13) | copy-start | bytes 3604
  37.0 11.4 %copy-start.2 = (bf16[3,3,300,300]{3,2,1,0:T(8,128)(2,1)S(1)}, bf16[3,3,300,300]{3,2,1,0:T(8,128)(2,1)}, u32[]{:S(2)}) copy-start(bf16[3,3,300,300]{3,2,1,0:T(8,128)(2,1)} %param.14) | copy-start | bytes 4860004
  37.1 7.5 %collective-permute-start.6 = (bf16[8,16,300]{2,1,0:T(8,128)(2,1)S(1)}, bf16[8,16,300]{2,1,0:T(8,128)(2,1)S(1)}, u32[]{:S(2)}, u32[]{:S(2)}) collective-permute-start(bf16[8,16,300]{2,1,0:T(8,128)(2,1)S(1)} %get-tuple-element.27), channel_id=1, source_target_pairs={{0,8},{8,16},{16,24},{24,0},{1,9},{9,17},{17,25},{25,1},{2,10},{10... | collective-permute-start | bytes 230408 | tf_op jit(solution)/shard_map/ppermute | solution.py:25
  38.4 7.1 %collective-permute-start.7 = (bf16[8,16,300]{2,1,0:T(8,128)(2,1)S(1)}, bf16[8,16,300]{2,1,0:T(8,128)(2,1)S(1)}, u32[]{:S(2)}, u32[]{:S(2)}) collective-permute-start(bf16[8,16,300]{2,1,0:T(8,128)(2,1)S(1)} %get-tuple-element.28), channel_id=1, source_target_pairs={{8,0},{16,8},{24,16},{0,24},{9,1},{17,9},{25,17},{1,25},{10,2},{18... | collective-permute-start | bytes 230408 | tf_op jit(solution)/shard_map/ppermute | solution.py:27
  45.7 9.9 %collective-permute-start.8 = (bf16[48,8,300]{2,1,0:T(8,128)(2,1)S(1)}, bf16[48,8,300]{2,1,0:T(8,128)(2,1)S(1)}, u32[]{:S(2)}, u32[]{:S(2)}) collective-permute-start(bf16[48,8,300]{2,1,0:T(8,128)(2,1)S(1)} %get-tuple-element.25), channel_id=1, source_target_pairs={{0,1},{1,2},{2,3},{3,4},{4,5},{5,6},{6,7},{7,0},{8,9},{9,10},{10,1... | collective-permute-start | bytes 691208 | tf_op jit(solution)/shard_map/ppermute | solution.py:25
  45.8 9.8 %collective-permute-start.9 = (bf16[48,8,300]{2,1,0:T(8,128)(2,1)S(1)}, bf16[48,8,300]{2,1,0:T(8,128)(2,1)S(1)}, u32[]{:S(2)}, u32[]{:S(2)}) collective-permute-start(bf16[48,8,300]{2,1,0:T(8,128)(2,1)S(1)} %get-tuple-element.26), channel_id=1, source_target_pairs={{1,0},{2,1},{3,2},{4,3},{5,4},{6,5},{7,6},{0,7},{9,8},{10,9},{11,1... | collective-permute-start | bytes 691208 | tf_op jit(solution)/shard_map/ppermute | solution.py:27
  58.3 1.4 %copy-start.8 = (f32[300]{0:T(512)S(1)}, f32[300]{0:T(512)}, u32[]{:S(2)}) copy-start(f32[300]{0:T(512)} %param.15) | copy-start | bytes 3604
where the time goes:
time: 63.1 us; the launch traced here: 62.8 us
  waiting for transfers between devices  20.1 us (32%)
  starting transfers between devices  18.1 us (29%)
  local copies, waits for them, and re-layouts  10.9 us (17%)
  other arithmetic  7.47 us (12%)
  matrix products  5.9 us (9%)
    ppermute x4, waiting for transfers between devices, padded(): lax.ppermute(tail, axis, [(i, (i + 1) % count) for i in range(count)])  14.6 us
    ppermute x4, starting transfers between devices, padded(): lax.ppermute(head, axis, [((i + 1) % count, i) for i in range(count)])  10.1 us
    dot_general x6, matrix products, dilated(): jnp.einsum('ijc,cd->ijd', band, taps, preferred_element_type=jnp.float32)  5.9 us
    ppermute x1, starting transfers between devices, shifted(): return lax.ppermute(block, axis, route)  4.92 us
    ppermute x1, waiting for transfers between devices, from_behind(): lax.ppermute(array, axis, [(i, (i + by) % devices) for i in range(devices)])  4.54 us
    mul x1, other arithmetic, on_device(): jax.nn.gelu(dilated(outer, w_two, b_two, 8, rows, cols), approximate=False)  3.13 us
    ppermute x4, starting transfers between devices, padded(): lax.ppermute(tail, axis, [(i, (i + 1) % count) for i in range(count)])  3.03 us
    convert_element_type x1, other arithmetic, on_device(): jax.nn.gelu(dilated(framed, w_one, b_one, 4, rows, cols), approximate=False)  2.65 us
  transfers between devices with their start and end apart: 10, of which 6 were waited for; matrix products, arithmetic and copies ran while one was open for 16% of the time, Pallas kernels for 0%

commit v1 on v0

v1 whole, which is shorter than its diff:
```python
import functools

import jax
import jax.numpy as jnp
from jax import lax
from jax.experimental import pallas as pl
from jax.experimental.pallas import tpu as pltpu
from jax.sharding import PartitionSpec as P

MESH = pl.DeviceIdType.MESH
SIDES = tuple((dp, dq) for dp in (-1, 0, 1) for dq in (-1, 0, 1) if (dp, dq) != (0, 0))
STEP = 4
LANES = 128


def gelu(x):
    return 0.5 * x * (1.0 + lax.erf(x * 0.7071067811865476))


def up_to(value, multiple):
    return -(-value // multiple) * multiple


def kernel(
    shape, fields, land, w_depth, b_depth, w_one, b_one, w_two, b_two, out,
    grid, edge, west, corner, mask, down, hidden, one, two, two_tail, result,
    load_sem, edge_sem, down_sem, hidden_sem, out_sem,
):
    n_lat, n_lon, rows, cols, chans, feats = shape
    bands, sectors = rows // STEP, cols // STEP
    main = feats // (2 * LANES) * (2 * LANES)
    tail = feats - main
    lat, lon = lax.axis_index("lat"), lax.axis_index("lon")
    has = {-1: lat > 0, 0: True, 1: lat < n_lat - 1}

    def when(dp, body):
        if dp == 0:
            body()
        else:
            pl.when(has[dp])(body)

    def device(dp, dq):
        return (lat + dp, lax.rem(lon + dq + n_lon, n_lon))

    halves = chans // LANES
    parts = [
        pltpu.make_async_copy(
            fields.at[:, :, h * LANES : (h + 1) * LANES], grid.at[h, 1:, 8:, :], load_sem.at[2 + h])
        for h in range(halves)
    ]
    load_one = pltpu.make_async_copy(w_one, one, load_sem.at[0])
    load_two = pltpu.make_async_copy(w_two, two, load_sem.at[1])
    for load in parts + [load_one, load_two]:
        load.start()

    barrier = pltpu.get_barrier_semaphore()
    for dp, dq in SIDES:
        when(dp, lambda dp=dp, dq=dq: pl.semaphore_signal(
            barrier, inc=1, device_id=device(dp, dq), device_id_type=MESH))

    cells = land[...].astype(jnp.float32)
    eye = lax.broadcasted_iota(jnp.int32, (cols, cols), 0) == lax.broadcasted_iota(
        jnp.int32, (cols, cols), 1)
    for i in range(rows):
        spread = jnp.where(eye, jnp.broadcast_to(cells[i : i + 1], (cols, cols)), 0.0)
        mask[i] = jnp.broadcast_to(jnp.sum(spread, axis=1, keepdims=True), mask.shape[1:])

    if tail:
        hidden[:, :, :, main:] = jnp.zeros(hidden.shape[:3] + (hidden.shape[3] - main,), hidden.dtype)

    def clear(buffer, width):
        gap = jnp.zeros((width,) + buffer.shape[1:], buffer.dtype)

        def north():
            buffer[0:width] = gap

        def south():
            buffer[buffer.shape[0] - width :] = gap

        pl.when(lat == 0)(north)
        pl.when(lat == n_lat - 1)(south)

    clear(down, 1)
    clear(hidden, 2)

    for h in range(halves):
        parts[h].wait()
        for r in range(2 * rows):
            edge[h, r : r + 1, :] = grid[h, 1 + r, 8 + 2 * cols - 1 : 8 + 2 * cols, :]

    pl.semaphore_wait(barrier, 2 + 3 * jnp.minimum(lat, 1) + 3 * jnp.minimum(n_lat - 1 - lat, 1))

    def remote(src, dst, sems, k, dp, dq):
        return pltpu.make_async_remote_copy(
            src_ref=src, dst_ref=dst, send_sem=sems.at[0, k], recv_sem=sems.at[1, k],
            device_id=device(dp, dq), device_id_type=MESH)

    last_row = remote(grid.at[:, 2 * rows, 8:, :], grid.at[:, 0, 8:, :], edge_sem, 0, 1, 0)
    last_col = remote(edge, west, edge_sem, 1, 0, 1)
    last_cell = remote(edge.at[:, 2 * rows - 8 :], corner, edge_sem, 2, 1, 1)
    last_col.start()

    def send_south():
        last_row.start()
        last_cell.start()

    when(1, send_south)

    def from_north():
        last_row.wait_recv()
        last_cell.wait_recv()
        for h in range(halves):
            grid[h, 0, 7:8, :] = corner[h, 7:8, :]

    def no_north():
        grid[:, 0] = jnp.zeros((halves,) + grid.shape[2:], grid.dtype)

    last_col.wait_recv()
    for h in range(halves):
        for r in range(2 * rows):
            grid[h, 1 + r, 7:8, :] = west[h, r : r + 1, :]
    pl.when(has[-1])(from_north)
    pl.when(lat == 0)(no_north)

    def down_band(p, carry):
        lines = []
        for r in range(STEP):
            i = STEP * p + r
            line = []
            for h in range(halves):
                lanes = slice(h * LANES, (h + 1) * LANES)
                total = jnp.broadcast_to(b_depth[:, lanes], (cols, LANES))
                for a in range(3):
                    for b in range(3):
                        piece = grid[h, 2 * i + a, pl.ds(7 + b, cols, stride=2), :]
                        total = total + piece * w_depth[a, b : b + 1, lanes]
                line.append(total * mask[i][:, :LANES])
            lines.append(jnp.concatenate(line, axis=1))
        for q in range(sectors):
            block = jnp.concatenate([line[STEP * q : STEP * q + STEP] for line in lines], axis=0)
            down[1 + p, 1 + q] = block.astype(down.dtype)
        return carry

    lax.fori_loop(0, bands, down_band, 0)

    def exchange(buffer, width, sems):
        def part(d, count, target):
            if d == 0:
                return slice(width, width + count)
            if (d > 0) != target:
                return slice(count, count + width) if d > 0 else slice(count + width, count + 2 * width)
            return slice(0, width) if target else slice(width, 2 * width)

        copies = []
        for k, (dp, dq) in enumerate(SIDES):
            src = buffer.at[part(dp, bands, False), part(dq, sectors, False)]
            dst = buffer.at[part(dp, bands, True), part(dq, sectors, True)]
            copies.append((dp, remote(src, dst, sems, k, dp, dq)))
        return copies

    def start(copies):
        for dp, copy in copies:
            when(dp, copy.start)

    def arrive(copies):
        for dp, copy in copies:
            when(-dp, copy.wait_recv)

    moves = exchange(down, 1, down_sem)
    start(moves)
    load_one.wait()
    load_two.wait()
    if tail:
        for t in range(9):
            two_tail[t] = jnp.zeros(two_tail.shape[1:], two_tail.dtype)
            two_tail[t, 0:tail, :] = two[t // 3, t % 3, main:feats, :]
    arrive(moves)

    chunk = bands // 2
    flat = chunk * sectors * STEP * STEP

    def first(c, carry):
        p = c * chunk
        pieces = [
            down[pl.ds(p + a, chunk), b : b + sectors].reshape(flat, chans)
            for a in range(3) for b in range(3)
        ]
        total = jnp.dot(
            jnp.concatenate(pieces, axis=1), one[...].reshape(9 * chans, feats),
            preferred_element_type=jnp.float32)
        value = gelu(total + b_one[...]).astype(hidden.dtype)
        hidden[pl.ds(2 + p, chunk), 2 : 2 + sectors, :, 0:feats] = value.reshape(
            chunk, sectors, STEP * STEP, feats)
        return carry

    lax.fori_loop(0, 2, first, 0)

    moves_two = exchange(hidden, 2, hidden_sem)
    start(moves_two)
    arrive(moves_two)

    def second(c, carry):
        p = c * chunk
        taps = [(a, b) for a in range(3) for b in range(3)]
        total = jnp.dot(
            jnp.concatenate(
                [hidden[pl.ds(p + 2 * a, chunk), 2 * b : 2 * b + sectors, :, 0:main].reshape(flat, main)
                 for a, b in taps], axis=1),
            jnp.concatenate([two[a, b, 0:main, :] for a, b in taps], axis=0),
            preferred_element_type=jnp.float32)
        if tail:
            extra = hidden.shape[3] - main
            total = total + jnp.dot(
                jnp.concatenate(
                    [hidden[pl.ds(p + 2 * a, chunk), 2 * b : 2 * b + sectors, :, main:].reshape(flat, extra)
                     for a, b in taps], axis=1),
                two_tail[...].reshape(9 * extra, feats),
                preferred_element_type=jnp.float32)
        value = gelu(total + b_two[...]).reshape(chunk, sectors, STEP * STEP, feats)
        for k in range(chunk):
            for r in range(STEP):
                line = jnp.concatenate(
                    [value[k, q, STEP * r : STEP * r + STEP] for q in range(sectors)], axis=0)
                i = STEP * (p + k) + r
                result[i] = line * mask[i][:, :feats]
        return carry

    lax.fori_loop(0, 2, second, 0)
    store = pltpu.make_async_copy(result, out, out_sem.at[0])
    store.start()

    last_col.wait_send()

    def sent_south():
        last_row.wait_send()
        last_cell.wait_send()

    when(1, sent_south)
    for dp, copy in moves + moves_two:
        when(dp, copy.wait_send)
    store.wait()


def on_device(n_lat, n_lon, fields, land_sea, w_depth, b_depth, w_one, b_one, w_two, b_two):
    rows, cols = land_sea.shape
    chans, feats = w_one.shape[2:]
    bands, sectors = rows // STEP, cols // STEP
    main = feats // (2 * LANES) * (2 * LANES)
    wide = up_to(feats, LANES)
    halves = chans // LANES
    any_space = pl.BlockSpec(memory_space=pl.ANY)
    vmem = pl.BlockSpec(memory_space=pltpu.VMEM)
    return pl.pallas_call(
        functools.partial(kernel, (n_lat, n_lon, rows, cols, chans, feats)),
        out_shape=jax.ShapeDtypeStruct((rows, cols, feats), jnp.float32),
        in_specs=[any_space, vmem, vmem, vmem, any_space, vmem, any_space, vmem],
        out_specs=any_space,
        scratch_shapes=[
            pltpu.VMEM((halves, 2 * rows + 1, 2 * cols + 8, LANES), jnp.float32),
            pltpu.VMEM((halves, 2 * rows, LANES), jnp.float32),
            pltpu.VMEM((halves, 2 * rows, LANES), jnp.float32),
            pltpu.VMEM((halves, 8, LANES), jnp.float32),
            pltpu.VMEM((rows, cols, wide), jnp.float32),
            pltpu.VMEM((bands + 2, sectors + 2, STEP * STEP, chans), jnp.bfloat16),
            pltpu.VMEM((bands + 4, sectors + 4, STEP * STEP, wide), jnp.bfloat16),
            pltpu.VMEM(w_one.shape, jnp.bfloat16),
            pltpu.VMEM(w_two.shape, jnp.bfloat16),
            pltpu.VMEM((9, max(wide - main, LANES), feats), jnp.bfloat16),
            pltpu.VMEM((rows, cols, feats), jnp.float32),
            pltpu.SemaphoreType.DMA((2 + halves,)),
            pltpu.SemaphoreType.DMA((2, 3)),
            pltpu.SemaphoreType.DMA((2, len(SIDES))),
            pltpu.SemaphoreType.DMA((2, len(SIDES))),
            pltpu.SemaphoreType.DMA((1,)),
        ],
        compiler_params=pltpu.CompilerParams(
            collective_id=0, has_side_effects=True, vmem_limit_bytes=40 * 1024 * 1024),
    )(fields, land_sea, w_depth, b_depth.reshape(1, chans), w_one, b_one.reshape(1, feats),
      w_two, b_two.reshape(1, feats))


def solution(mesh):
    return jax.shard_map(
        functools.partial(on_device, mesh.shape["lat"], mesh.shape["lon"]),
        mesh=mesh,
        in_specs=(P("lat", "lon", None), P("lat", "lon"), P(), P(), P(), P(), P(), P()),
        out_specs=P("lat", "lon", None),
        check_vma=False,
    )
```

time: 63.1 us -> 33.3 us (0.53)
  Pallas kernels: 0 us -> 24 us
  waiting for transfers between devices: 20.1 us -> 0 us
  starting transfers between devices: 18.1 us -> 0 us
  other arithmetic: 7.47 us -> 0 us
  matrix products: 5.9 us -> 0 us
  local copies, waits for them, and re-layouts: 10.9 us -> 8.9 us
    pallas_call x0 -> x1, Pallas kernels: none -> 24 us  [on_device(): pl.pallas_call(functools.partial(kernel, (n_lat, n_lon, rows, cols, chans...]
    ppermute x10 -> x0, waiting for transfers between devices: 20.1 us -> none  [the longest x4 14.6 us: padded(): lax.ppermute(tail, axis, [(i, (i + 1) % count) for i in range(count)])]
    ppermute x10 -> x0, starting transfers between devices: 18.1 us -> none  [the longest x4 10.1 us: padded(): lax.ppermute(head, axis, [((i + 1) % count, i) for i in range(count)])]
    unnamed x21 -> x11, local copies, waits for them, and re-layouts: 1.52 us -> 7.51 us
    dot_general x6 -> x0, matrix products: 5.9 us -> none  [dilated(): jnp.einsum('ijc,cd->ijd', band, taps, preferred_element_type=jnp.float32)]
    slice x10 -> x0, local copies, waits for them, and re-layouts: 4.57 us -> none  [the longest x1 1.29 us: on_device(): rows_odd[:-1]]
    convert_element_type x3 -> x0, other arithmetic: 4.05 us -> none  [the longest x1 2.65 us: on_device(): jax.nn.gelu(dilated(framed, w_one, b_one, 4, rows, cols), approximate=False)]
    mul x1 -> x0, other arithmetic: 3.13 us -> none  [on_device(): jax.nn.gelu(dilated(outer, w_two, b_two, 8, rows, cols), approximate=False)]
  transfers between devices with their start and end apart: 10 -> 0, of which waited for: 6 -> 0; matrix products, arithmetic and copies ran while one was open for 16% -> 0% of each run, Pallas kernels for 0% -> 0%
where the time goes in v1:
time: 33.3 us; the launch traced here: 33 us
  Pallas kernels  24 us (72%)
  local copies, waits for them, and re-layouts  8.9 us (27%)
    pallas_call x1, Pallas kernels, on_device(): pl.pallas_call(functools.partial(kernel, (n_lat, n_lon, rows, cols, chans...  24 us
    unnamed x11, local copies, waits for them, and re-layouts  7.51 us
    reshape x1, local copies, waits for them, and re-layouts, on_device(): b_one.reshape(1, feats)  0.71 us
    reshape x1, local copies, waits for them, and re-layouts, on_device(): b_two.reshape(1, feats)  0.68 us

profile of v1, /device:TPU:0, one launch (start us, length us, event | category | flops | bytes accessed | tf_op | source)
XLA Modules:
  0.0 33.0 jit_solution(2554479620689921082)
XLA Ops:
  0.0 0.0 copy-start.3
  0.0 0.0 copy-start.2
  0.0 0.7 %reshape.10.b_one = f32[1,300]{1,0:T(1,128)S(1)} reshape(f32[300]{0:T(512)} %param.13) | data formatting | bytes 2400 | tf_op jit(solution)/shard_map/reshape | solution.py:278
  0.7 0.7 %reshape.11.b_two = f32[1,300]{1,0:T(1,128)S(1)} reshape(f32[300]{0:T(512)} %param.15) | data formatting | bytes 2400 | tf_op jit(solution)/shard_map/reshape | solution.py:279
  1.4 0.8 %copy.9.land = s32[32,16]{1,0:T(8,128)S(1)} copy(s32[32,16]{0,1:T(8,128)} %param.9) | data formatting | bytes 4096 | tf_op args[1]
  2.2 2.7 %copy.10.w_one = bf16[3,3,256,300]{3,2,1,0:T(8,128)(2,1)S(1)} copy(bf16[3,3,256,300]{2,3,1,0:T(8,128)(2,1)} %param.12) | data formatting | bytes 2764800 | tf_op args[4]
  4.8 0.0 copy-done.3
  4.9 0.0 copy-done.2
  4.9 0.0 copy-start
  4.9 1.6 %copy-done = bf16[3,3,300,300]{3,2,1,0:T(8,128)(2,1)S(1)} copy-done((bf16[3,3,300,300]{3,2,1,0:T(8,128)(2,1)S(1)}, bf16[3,3,300,300]{3,2,1,0:T(8,128)(2,1)}, u32[]{:S(2)}) %copy-start) | copy-done | bytes 1620024
  6.5 0.0 copy-start.1
  6.5 1.6 %copy-done.1 = f32[64,32,256]{2,1,0:T(8,128)S(1)} copy-done((f32[64,32,256]{2,1,0:T(8,128)S(1)}, f32[64,32,256]{2,1,0:T(8,128)}, u32[]{:S(2)}) %copy-start.1) | copy-done | bytes 2097176
  8.1 24.0 %shard_map.82 = f32[32,16,300]{2,1,0:T(8,128)S(1)} custom-call(f32[64,32,256]{2,1,0:T(8,128)S(1)} %copy-done.1, s32[32,16]{1,0:T(8,128)S(1)} %copy.9.land, f32[3,3,256]{2,1,0:T(4,128)S(1)} %copy-done.2, f32[1,256]{1,0:T(1,128)S(1)} %bitcast.1, bf16[3,3,256,300]{3,2,1,0:T(8,128)(2,1)S(1)} %copy.10.w_one, f32[1,300]{1,0:T(1,128)S(1)} %reshape.10.b_one, ...), custom_call_target="tpu_custom_call" | custom-call | tf_op jit(solution)/shard_map/pallas_call | solution.py:253
  32.1 0.9 %copy.12 = f32[32,16,300]{2,1,0:T(8,128)} copy(f32[32,16,300]{2,1,0:T(8,128)S(1)} %shard_map.82) | data formatting | bytes 1228800
Async XLA Ops:
  0.0 4.8 %copy-start.3 = (f32[256]{0:T(256)S(1)}, f32[256]{0:T(256)}, u32[]{:S(2)}) copy-start(f32[256]{0:T(256)} %param.11) | copy-start | bytes 3076
  0.0 4.9 %copy-start.2 = (f32[3,3,256]{2,1,0:T(4,128)S(1)}, f32[3,3,256]{2,1,0:T(4,128)}, u32[]{:S(2)}) copy-start(f32[3,3,256]{2,1,0:T(4,128)} %w_depth.1) | copy-start | bytes 27652
  4.9 1.6 %copy-start = (bf16[3,3,300,300]{3,2,1,0:T(8,128)(2,1)S(1)}, bf16[3,3,300,300]{3,2,1,0:T(8,128)(2,1)}, u32[]{:S(2)}) copy-start(bf16[3,3,300,300]{3,2,1,0:T(8,128)(2,1)} %w_two.1) | copy-start | bytes 4860004
  6.5 1.6 %copy-start.1 = (f32[64,32,256]{2,1,0:T(8,128)S(1)}, f32[64,32,256]{2,1,0:T(8,128)}, u32[]{:S(2)}) copy-start(f32[64,32,256]{2,1,0:T(8,128)} %fields.1) | copy-start | bytes 6291460

commit v2 on v1

--- a/solution.py
+++ b/solution.py
@@ -23,7 +23,7 @@
 
 def kernel(
     shape, fields, land, w_depth, b_depth, w_one, b_one, w_two, b_two, out,
-    grid, edge, west, corner, mask, down, hidden, one, two, two_tail, result,
+    grid, edge, west, corner, late, open_block, open_sea, mask, down, hidden, one, two, two_tail, result,
     load_sem, edge_sem, down_sem, hidden_sem, out_sem,
 ):
     n_lat, n_lon, rows, cols, chans, feats = shape
@@ -59,11 +59,8 @@
             barrier, inc=1, device_id=device(dp, dq), device_id_type=MESH))
 
     cells = land[...].astype(jnp.float32)
-    eye = lax.broadcasted_iota(jnp.int32, (cols, cols), 0) == lax.broadcasted_iota(
-        jnp.int32, (cols, cols), 1)
     for i in range(rows):
-        spread = jnp.where(eye, jnp.broadcast_to(cells[i : i + 1], (cols, cols)), 0.0)
-        mask[i] = jnp.broadcast_to(jnp.sum(spread, axis=1, keepdims=True), mask.shape[1:])
+        mask[i] = jnp.broadcast_to(cells[:, i : i + 1], mask.shape[1:])
 
     if tail:
         hidden[:, :, :, main:] = jnp.zeros(hidden.shape[:3] + (hidden.shape[3] - main,), hidden.dtype)
@@ -80,6 +77,10 @@
         pl.when(lat == 0)(north)
         pl.when(lat == n_lat - 1)(south)
 
+    def no_north():
+        grid[:, 0, 8:, :] = jnp.zeros((halves, 2 * cols, LANES), grid.dtype)
+
+    pl.when(lat == 0)(no_north)
     clear(down, 1)
     clear(hidden, 2)
 
@@ -115,33 +116,65 @@
     def no_north():
         grid[:, 0] = jnp.zeros((halves,) + grid.shape[2:], grid.dtype)
 
+    for h in range(halves):
+        grid[h, :, 0:8, :] = jnp.zeros((2 * rows + 1, 8, LANES), grid.dtype)
+        late[h] = jnp.zeros(late.shape[1:], late.dtype)
+
+    def down_line(i):
+        line = []
+        for h in range(halves):
+            lanes = slice(h * LANES, (h + 1) * LANES)
+            total = jnp.broadcast_to(b_depth[...].reshape(1, chans)[:, lanes], (cols, LANES))
+            for a in range(3):
+                for b in range(3):
+                    piece = grid[h, 2 * i + a, pl.ds(7 + b, cols, stride=2), :]
+                    total = total + piece * w_depth[a, b : b + 1, lanes]
+            line.append(total)
+        return jnp.concatenate(line, axis=1)
+
+    def gather(lines, q):
+        return jnp.concatenate([line[STEP * q : STEP * q + STEP] for line in lines], axis=0)
+
+    def down_band(p):
+        lines = [down_line(STEP * p + r) for r in range(STEP)]
+        seas = [mask[STEP * p + r][:, :chans] for r in range(STEP)]
+        masked = [line * sea for line, sea in zip(lines, seas)]
+        for q in range(1, sectors):
+            down[1 + p, 1 + q] = gather(masked, q).astype(down.dtype)
+        return gather(lines, 0), gather(seas, 0)
+
+    def later_band(p, carry):
+        block, sea = down_band(p)
+        open_block[p] = block
+        open_sea[p] = sea
+        return carry
+
+    lax.fori_loop(1, bands, later_band, 0)
+
     last_col.wait_recv()
     for h in range(halves):
-        for r in range(2 * rows):
+        lanes = slice(h * LANES, (h + 1) * LANES)
+        from_west = sum(
+            west[h, pl.ds(8 * STEP // 4 - 1 + a, rows - STEP, stride=2), :] * w_depth[a, 0:1, lanes]
+            for a in range(3))
+        late[h, pl.ds(STEP * STEP, rows - STEP, stride=STEP), :] = from_west
+    for p in range(1, bands):
+        extra = jnp.concatenate(
+            [late[h, STEP * STEP * p : STEP * STEP * (p + 1), :] for h in range(halves)], axis=1)
+        down[1 + p, 1] = ((open_block[p] + extra) * open_sea[p]).astype(down.dtype)
+
+    def from_north():
+        last_row.wait_recv()
+        last_cell.wait_recv()
+        for h in range(halves):
+            grid[h, 0, 7:8, :] = corner[h, 7:8, :]
+
+    for h in range(halves):
+        for r in range(2 * STEP):
             grid[h, 1 + r, 7:8, :] = west[h, r : r + 1, :]
     pl.when(has[-1])(from_north)
-    pl.when(lat == 0)(no_north)
-
-    def down_band(p, carry):
-        lines = []
-        for r in range(STEP):
-            i = STEP * p + r
-            line = []
-            for h in range(halves):
-                lanes = slice(h * LANES, (h + 1) * LANES)
-                total = jnp.broadcast_to(b_depth[:, lanes], (cols, LANES))
-                for a in range(3):
-                    for b in range(3):
-                        piece = grid[h, 2 * i + a, pl.ds(7 + b, cols, stride=2), :]
-                        total = total + piece * w_depth[a, b : b + 1, lanes]
-                line.append(total * mask[i][:, :LANES])
-            lines.append(jnp.concatenate(line, axis=1))
-        for q in range(sectors):
-            block = jnp.concatenate([line[STEP * q : STEP * q + STEP] for line in lines], axis=0)
-            down[1 + p, 1 + q] = block.astype(down.dtype)
-        return carry
-
-    lax.fori_loop(0, bands, down_band, 0)
+    block, sea = down_band(0)
+    down[1, 1] = (block * sea).astype(down.dtype)
 
     def exchange(buffer, width, sems):
         def part(d, count, target):
@@ -185,10 +218,11 @@
             down[pl.ds(p + a, chunk), b : b + sectors].reshape(flat, chans)
             for a in range(3) for b in range(3)
         ]
-        total = jnp.dot(
-            jnp.concatenate(pieces, axis=1), one[...].reshape(9 * chans, feats),
-            preferred_element_type=jnp.float32)
-        value = gelu(total + b_one[...]).astype(hidden.dtype)
+        total = lax.dot_general(
+            jnp.concatenate(pieces, axis=1),
+            jnp.concatenate([one[a, b] for a in range(3) for b in range(3)], axis=1),
+            (((1,), (1,)), ((), ())), preferred_element_type=jnp.float32)
+        value = gelu(total + b_one[...].reshape(1, feats)).astype(hidden.dtype)
         hidden[pl.ds(2 + p, chunk), 2 : 2 + sectors, :, 0:feats] = value.reshape(
             chunk, sectors, STEP * STEP, feats)
         return carry
@@ -216,7 +250,7 @@
                      for a, b in taps], axis=1),
                 two_tail[...].reshape(9 * extra, feats),
                 preferred_element_type=jnp.float32)
-        value = gelu(total + b_two[...]).reshape(chunk, sectors, STEP * STEP, feats)
+        value = gelu(total + b_two[...].reshape(1, feats)).reshape(chunk, sectors, STEP * STEP, feats)
         for k in range(chunk):
             for r in range(STEP):
                 line = jnp.concatenate(
@@ -248,6 +282,7 @@
     main = feats // (2 * LANES) * (2 * LANES)
     wide = up_to(feats, LANES)
     halves = chans // LANES
+    taps_out_in = jnp.swapaxes(w_one, 2, 3)
     any_space = pl.BlockSpec(memory_space=pl.ANY)
     vmem = pl.BlockSpec(memory_space=pltpu.VMEM)
     return pl.pallas_call(
@@ -260,10 +295,13 @@
             pltpu.VMEM((halves, 2 * rows, LANES), jnp.float32),
             pltpu.VMEM((halves, 2 * rows, LANES), jnp.float32),
             pltpu.VMEM((halves, 8, LANES), jnp.float32),
+            pltpu.VMEM((halves, STEP * rows, LANES), jnp.float32),
+            pltpu.VMEM((bands, STEP * STEP, chans), jnp.float32),
+            pltpu.VMEM((bands, STEP * STEP, chans), jnp.float32),
             pltpu.VMEM((rows, cols, wide), jnp.float32),
             pltpu.VMEM((bands + 2, sectors + 2, STEP * STEP, chans), jnp.bfloat16),
             pltpu.VMEM((bands + 4, sectors + 4, STEP * STEP, wide), jnp.bfloat16),
-            pltpu.VMEM(w_one.shape, jnp.bfloat16),
+            pltpu.VMEM(taps_out_in.shape, jnp.bfloat16),
             pltpu.VMEM(w_two.shape, jnp.bfloat16),
             pltpu.VMEM((9, max(wide - main, LANES), feats), jnp.bfloat16),
             pltpu.VMEM((rows, cols, feats), jnp.float32),
@@ -274,9 +312,8 @@
             pltpu.SemaphoreType.DMA((1,)),
         ],
         compiler_params=pltpu.CompilerParams(
-            collective_id=0, has_side_effects=True, vmem_limit_bytes=40 * 1024 * 1024),
-    )(fields, land_sea, w_depth, b_depth.reshape(1, chans), w_one, b_one.reshape(1, feats),
-      w_two, b_two.reshape(1, feats))
+            collective_id=0, has_side_effects=True, vmem_limit_bytes=62 * 1024 * 1024),
+    )(fields, land_sea.T, w_depth, b_depth, taps_out_in, b_one, w_two, b_two)
 
 
 def solution(mesh):

time: 33.3 us -> 26.8 us (0.80)
  local copies, waits for them, and re-layouts: 8.9 us -> 2.06 us
  Pallas kernels: 24 us -> 24.5 us
    unnamed x11 -> x1, local copies, waits for them, and re-layouts: 7.51 us -> 2.06 us
    reshape x2 -> x0, local copies, waits for them, and re-layouts: 1.39 us -> none  [the longest x1 0.71 us: on_device(): b_one.reshape(1, feats)]
    pallas_call x1, Pallas kernels: 24 us -> 24.5 us  [on_device(): pl.pallas_call(functools.partial(kernel, (n_lat, n_lon, rows, cols, chans...]
where the time goes in v2:
time: 26.8 us; the launch traced here: 26.6 us
  Pallas kernels  24.5 us (91%)
  local copies, waits for them, and re-layouts  2.06 us (8%)
    pallas_call x1, Pallas kernels, on_device(): pl.pallas_call(functools.partial(kernel, (n_lat, n_lon, rows, cols, chans...  24.5 us
    unnamed x1, local copies, waits for them, and re-layouts  2.06 us

profile of v2, /device:TPU:0, one launch (start us, length us, event | category | flops | bytes accessed | tf_op | source)
XLA Modules:
  0.0 26.6 jit_solution(6229871915339404785)
XLA Ops:
  0.0 24.5 %shard_map.82 = f32[32,16,300]{2,1,0:T(8,128)} custom-call(f32[64,32,256]{2,1,0:T(8,128)} %fields.1, s32[16,32]{1,0:T(8,128)} %bitcast.3, f32[3,3,256]{2,1,0:T(4,128)} %w_depth.1, f32[256]{0:T(256)} %b_depth.1, bf16[3,3,300,256]{3,2,1,0:T(8,128)(2,1)} %bitcast.2, f32[300]{0:T(512)} %b_one.1, bf16[3,3,300,300]{3,2,1,0:T(8,128)(2,1)} %w_two.1, f32[300]{0:T(512)} %b_two.1), custom_call_target="tpu_custom_call" | custom-call | tf_op jit(solution)/shard_map/pallas_call | solution.py:288
  24.5 2.1 %copy.10 = f32[32,16,300]{2,1,0:T(8,128)} copy(f32[32,16,300]{2,1,0:T(8,128)} %shard_map.82) | data formatting | bytes 1228800

commit v3 on v2

--- a/solution.py
+++ b/solution.py
@@ -23,8 +23,8 @@
 
 def kernel(
     shape, fields, land, w_depth, b_depth, w_one, b_one, w_two, b_two, out,
-    grid, edge, west, corner, late, open_block, open_sea, mask, down, hidden, one, two, two_tail, result,
-    load_sem, edge_sem, down_sem, hidden_sem, out_sem,
+    grid, edge, west, corner, late, open_block, open_sea, mask, down, hidden, one, two, two_tail, from_n, from_s, from_w, from_e, sums,
+    load_sem, edge_sem, down_sem, hidden_sem,
 ):
     n_lat, n_lon, rows, cols, chans, feats = shape
     bands, sectors = rows // STEP, cols // STEP
@@ -43,14 +43,19 @@
         return (lat + dp, lax.rem(lon + dq + n_lon, n_lon))
 
     halves = chans // LANES
-    parts = [
-        pltpu.make_async_copy(
-            fields.at[:, :, h * LANES : (h + 1) * LANES], grid.at[h, 1:, 8:, :], load_sem.at[2 + h])
-        for h in range(halves)
-    ]
+    split = 2 * cols - 8
+
+    def part(h, k):
+        start, size = ((split, 8), (0, split))[k]
+        return pltpu.make_async_copy(
+            fields.at[:, start : start + size, h * LANES : (h + 1) * LANES],
+            grid.at[h, 1:, 8 + start : 8 + start + size, :], load_sem.at[2 + 2 * h + k])
+
+    edge_parts = [part(h, 0) for h in range(halves)]
+    inner_parts = [part(h, 1) for h in range(halves)]
     load_one = pltpu.make_async_copy(w_one, one, load_sem.at[0])
     load_two = pltpu.make_async_copy(w_two, two, load_sem.at[1])
-    for load in parts + [load_one, load_two]:
+    for load in edge_parts + inner_parts:
         load.start()
 
     barrier = pltpu.get_barrier_semaphore()
@@ -62,8 +67,8 @@
     for i in range(rows):
         mask[i] = jnp.broadcast_to(cells[:, i : i + 1], mask.shape[1:])
 
-    if tail:
-        hidden[:, :, :, main:] = jnp.zeros(hidden.shape[:3] + (hidden.shape[3] - main,), hidden.dtype)
+    for p in range(bands + 4):
+        hidden[p] = jnp.zeros(hidden.shape[1:], hidden.dtype)
 
     def clear(buffer, width):
         gap = jnp.zeros((width,) + buffer.shape[1:], buffer.dtype)
@@ -82,10 +87,23 @@
 
     pl.when(lat == 0)(no_north)
     clear(down, 1)
-    clear(hidden, 2)
+
+    def clear_far(lat_at, first, line):
+        def body():
+            for buffer in (from_w, from_e):
+                buffer[first : first + 2] = jnp.zeros((2,) + buffer.shape[1:], buffer.dtype)
+            line[:, 2 : 2 + sectors] = jnp.zeros((2, sectors) + line.shape[2:], line.dtype)
+
+        pl.when(lat == lat_at)(body)
+
+    clear_far(0, 0, from_n)
+    clear_far(n_lat - 1, bands + 2, from_s)
+    for line in (from_n, from_s):
+        for q in (0, 2 + sectors):
+            line[:, q : q + 2] = jnp.zeros((2, 2) + line.shape[2:], line.dtype)
 
     for h in range(halves):
-        parts[h].wait()
+        edge_parts[h].wait()
         for r in range(2 * rows):
             edge[h, r : r + 1, :] = grid[h, 1 + r, 8 + 2 * cols - 1 : 8 + 2 * cols, :]
 
@@ -100,12 +118,12 @@
     last_col = remote(edge, west, edge_sem, 1, 0, 1)
     last_cell = remote(edge.at[:, 2 * rows - 8 :], corner, edge_sem, 2, 1, 1)
     last_col.start()
-
-    def send_south():
-        last_row.start()
-        last_cell.start()
-
-    when(1, send_south)
+    when(1, last_cell.start)
+    for inner in inner_parts:
+        inner.wait()
+    when(1, last_row.start)
+    load_one.start()
+    load_two.start()
 
     def from_north():
         last_row.wait_recv()
@@ -229,39 +247,78 @@
 
     lax.fori_loop(0, 2, first, 0)
 
-    moves_two = exchange(hidden, 2, hidden_sem)
-    start(moves_two)
-    arrive(moves_two)
-
-    def second(c, carry):
-        p = c * chunk
-        taps = [(a, b) for a in range(3) for b in range(3)]
+    def side(k, dq, first, count):
+        buffer, q = (from_w, 2 + sectors - 2) if dq > 0 else (from_e, 2)
+        return remote(hidden.at[2 + first : 2 + first + count, q : q + 2],
+                      buffer.at[2 + first : 2 + first + count], hidden_sem, k, 0, dq)
+
+    outer = [side(0, 1, 0, 2), side(1, -1, 0, 2), side(2, 1, bands - 2, 2), side(3, -1, bands - 2, 2)]
+    inner = [side(4, 1, 2, bands - 4), side(5, -1, 2, bands - 4)]
+    own = slice(2, 2 + sectors)
+    lat_moves = [
+        (-1, remote(hidden.at[2:4, own], from_s.at[:, own], hidden_sem, 6, -1, 0)),
+        (1, remote(hidden.at[bands : bands + 2, own], from_n.at[:, own], hidden_sem, 7, 1, 0)),
+    ]
+    corners = [
+        (-1, remote(from_w.at[2:4], from_w.at[bands + 2 :], hidden_sem, 8, -1, 0)),
+        (-1, remote(from_e.at[2:4], from_e.at[bands + 2 :], hidden_sem, 9, -1, 0)),
+        (1, remote(from_w.at[bands : bands + 2], from_w.at[0:2], hidden_sem, 10, 1, 0)),
+        (1, remote(from_e.at[bands : bands + 2], from_e.at[0:2], hidden_sem, 11, 1, 0)),
+    ]
+    for copy in outer:
+        copy.start()
+    start(lat_moves)
+    for copy in inner:
+        copy.start()
+
+    def taps_of(buffer, places, taps, size):
+        count = size[0] * size[1] * STEP * STEP
+        window = [
+            buffer[pl.ds(p, size[0]), q : q + size[1]].reshape(count, buffer.shape[3])
+            for p, q in places
+        ]
         total = jnp.dot(
-            jnp.concatenate(
-                [hidden[pl.ds(p + 2 * a, chunk), 2 * b : 2 * b + sectors, :, 0:main].reshape(flat, main)
-                 for a, b in taps], axis=1),
+            jnp.concatenate([cells[:, 0:main] for cells in window], axis=1),
             jnp.concatenate([two[a, b, 0:main, :] for a, b in taps], axis=0),
             preferred_element_type=jnp.float32)
         if tail:
-            extra = hidden.shape[3] - main
             total = total + jnp.dot(
-                jnp.concatenate(
-                    [hidden[pl.ds(p + 2 * a, chunk), 2 * b : 2 * b + sectors, :, main:].reshape(flat, extra)
-                     for a, b in taps], axis=1),
-                two_tail[...].reshape(9 * extra, feats),
+                jnp.concatenate([cells[:, main:] for cells in window], axis=1),
+                jnp.concatenate([two_tail[3 * a + b] for a, b in taps], axis=0),
                 preferred_element_type=jnp.float32)
-        value = gelu(total + b_two[...].reshape(1, feats)).reshape(chunk, sectors, STEP * STEP, feats)
-        for k in range(chunk):
-            for r in range(STEP):
-                line = jnp.concatenate(
-                    [value[k, q, STEP * r : STEP * r + STEP] for q in range(sectors)], axis=0)
-                i = STEP * (p + k) + r
-                result[i] = line * mask[i][:, :feats]
+        return total.reshape(size + (STEP * STEP, feats))
+
+    every = [(a, b) for a in range(3) for b in range(3)]
+
+    def second(c):
+        p = c * chunk
+        sums[p : p + chunk] = taps_of(
+            hidden, [(p + 2 * a, 2 * b) for a, b in every], every, (chunk, sectors))
+
+    second(0)
+    for copy in outer:
+        copy.wait_recv()
+    start(corners)
+    second(1)
+    arrive(lat_moves)
+    sums[0:2] += taps_of(from_n, [(0, 2 * b) for b in range(3)], [(0, b) for b in range(3)], (2, sectors))
+    sums[bands - 2 :] += taps_of(
+        from_s, [(0, 2 * b) for b in range(3)], [(2, b) for b in range(3)], (2, sectors))
+    for copy in inner:
+        copy.wait_recv()
+    arrive(corners)
+    sums[:, 0:2] += taps_of(from_w, [(2 * a, 0) for a in range(3)], [(a, 0) for a in range(3)], (bands, 2))
+    sums[:, sectors - 2 :] += taps_of(
+        from_e, [(2 * a, 0) for a in range(3)], [(a, 2) for a in range(3)], (bands, 2))
+
+    def finish(p, carry):
+        value = gelu(sums[p] + b_two[...].reshape(1, 1, feats))
+        for r in range(STEP):
+            i = STEP * p + r
+            out[i] = gather([value[q, STEP * r : STEP * r + STEP] for q in range(sectors)], 0) * mask[i][:, :feats]
         return carry
 
-    lax.fori_loop(0, 2, second, 0)
-    store = pltpu.make_async_copy(result, out, out_sem.at[0])
-    store.start()
+    lax.fori_loop(0, bands, finish, 0)
 
     last_col.wait_send()
 
@@ -270,9 +327,10 @@
         last_cell.wait_send()
 
     when(1, sent_south)
-    for dp, copy in moves + moves_two:
+    for dp, copy in moves + lat_moves + corners:
         when(dp, copy.wait_send)
-    store.wait()
+    for copy in outer + inner:
+        copy.wait_send()
 
 
 def on_device(n_lat, n_lon, fields, land_sea, w_depth, b_depth, w_one, b_one, w_two, b_two):
@@ -283,13 +341,13 @@
     wide = up_to(feats, LANES)
     halves = chans // LANES
     taps_out_in = jnp.swapaxes(w_one, 2, 3)
-    any_space = pl.BlockSpec(memory_space=pl.ANY)
+    any_space = pl.BlockSpec(memory_space=pltpu.HBM)
     vmem = pl.BlockSpec(memory_space=pltpu.VMEM)
     return pl.pallas_call(
         functools.partial(kernel, (n_lat, n_lon, rows, cols, chans, feats)),
-        out_shape=jax.ShapeDtypeStruct((rows, cols, feats), jnp.float32),
+        out_shape=pltpu.VMEM((rows, cols, feats), jnp.float32),
         in_specs=[any_space, vmem, vmem, vmem, any_space, vmem, any_space, vmem],
-        out_specs=any_space,
+        out_specs=vmem,
         scratch_shapes=[
             pltpu.VMEM((halves, 2 * rows + 1, 2 * cols + 8, LANES), jnp.float32),
             pltpu.VMEM((halves, 2 * rows, LANES), jnp.float32),
@@ -304,12 +362,15 @@
             pltpu.VMEM(taps_out_in.shape, jnp.bfloat16),
             pltpu.VMEM(w_two.shape, jnp.bfloat16),
             pltpu.VMEM((9, max(wide - main, LANES), feats), jnp.bfloat16),
-            pltpu.VMEM((rows, cols, feats), jnp.float32),
-            pltpu.SemaphoreType.DMA((2 + halves,)),
+            pltpu.VMEM((2, sectors + 4, STEP * STEP, wide), jnp.bfloat16),
+            pltpu.VMEM((2, sectors + 4, STEP * STEP, wide), jnp.bfloat16),
+            pltpu.VMEM((bands + 4, 2, STEP * STEP, wide), jnp.bfloat16),
+            pltpu.VMEM((bands + 4, 2, STEP * STEP, wide), jnp.bfloat16),
+            pltpu.VMEM((bands, sectors, STEP * STEP, feats), jnp.float32),
+            pltpu.SemaphoreType.DMA((2 + 2 * halves,)),
             pltpu.SemaphoreType.DMA((2, 3)),
             pltpu.SemaphoreType.DMA((2, len(SIDES))),
-            pltpu.SemaphoreType.DMA((2, len(SIDES))),
-            pltpu.SemaphoreType.DMA((1,)),
+            pltpu.SemaphoreType.DMA((2, 12)),
         ],
         compiler_params=pltpu.CompilerParams(
             collective_id=0, has_side_effects=True, vmem_limit_bytes=62 * 1024 * 1024),

time: 26.8 us -> 24.5 us (0.914)
  local copies, waits for them, and re-layouts: 2.06 us -> 0.88 us
  Pallas kernels: 24.5 us -> 23.4 us
    unnamed x1, local copies, waits for them, and re-layouts: 2.06 us -> 0.88 us
    pallas_call x1, Pallas kernels: 24.5 us -> 23.4 us  [on_device(): pl.pallas_call(functools.partial(kernel, (n_lat, n_lon, rows, cols, chans...]
where the time goes in v3:
time: 24.5 us; the launch traced here: 24.3 us
  Pallas kernels  23.4 us (96%)
  local copies, waits for them, and re-layouts  0.88 us (4%)
    pallas_call x1, Pallas kernels, on_device(): pl.pallas_call(functools.partial(kernel, (n_lat, n_lon, rows, cols, chans...  23.4 us
    unnamed x1, local copies, waits for them, and re-layouts  0.88 us

profile of v3, /device:TPU:0, one launch (start us, length us, event | category | flops | bytes accessed | tf_op | source)
XLA Modules:
  0.0 24.3 jit_solution(13687491241679598739)
XLA Ops:
  0.0 23.4 %shard_map.82 = f32[32,16,300]{2,1,0:T(8,128)S(1)} custom-call(f32[64,32,256]{2,1,0:T(8,128)} %fields.1, s32[16,32]{1,0:T(8,128)} %bitcast.3, f32[3,3,256]{2,1,0:T(4,128)} %w_depth.1, f32[256]{0:T(256)} %b_depth.1, bf16[3,3,300,256]{3,2,1,0:T(8,128)(2,1)} %bitcast.2, f32[300]{0:T(512)} %b_one.1, bf16[3,3,300,300]{3,2,1,0:T(8,128)(2,1)} %w_two.1, f32[300]{0:T(512)} %b_two.1), custom_call_target="tpu_custom_call" | custom-call | tf_op jit(solution)/shard_map/pallas_call | solution.py:346
  23.4 0.9 %copy.10 = f32[32,16,300]{2,1,0:T(8,128)} copy(f32[32,16,300]{2,1,0:T(8,128)S(1)} %shard_map.82) | data formatting | bytes 1228800

commit v4 on v3

--- a/solution.py
+++ b/solution.py
@@ -23,8 +23,8 @@
 
 def kernel(
     shape, fields, land, w_depth, b_depth, w_one, b_one, w_two, b_two, out,
-    grid, edge, west, corner, late, open_block, open_sea, mask, down, hidden, one, two, two_tail, from_n, from_s, from_w, from_e, sums,
-    load_sem, edge_sem, down_sem, hidden_sem,
+    grid, edge, west, corner, late, open_block, open_sea, mask, down, hidden, one, two, two_tail, sums,
+    load_sem, edge_sem, down_sem,
 ):
     n_lat, n_lon, rows, cols, chans, feats = shape
     bands, sectors = rows // STEP, cols // STEP
@@ -86,21 +86,7 @@
         grid[:, 0, 8:, :] = jnp.zeros((halves, 2 * cols, LANES), grid.dtype)
 
     pl.when(lat == 0)(no_north)
-    clear(down, 1)
-
-    def clear_far(lat_at, first, line):
-        def body():
-            for buffer in (from_w, from_e):
-                buffer[first : first + 2] = jnp.zeros((2,) + buffer.shape[1:], buffer.dtype)
-            line[:, 2 : 2 + sectors] = jnp.zeros((2, sectors) + line.shape[2:], line.dtype)
-
-        pl.when(lat == lat_at)(body)
-
-    clear_far(0, 0, from_n)
-    clear_far(n_lat - 1, bands + 2, from_s)
-    for line in (from_n, from_s):
-        for q in (0, 2 + sectors):
-            line[:, q : q + 2] = jnp.zeros((2, 2) + line.shape[2:], line.dtype)
+    clear(down, 3)
 
     for h in range(halves):
         edge_parts[h].wait()
@@ -124,15 +110,6 @@
     when(1, last_row.start)
     load_one.start()
     load_two.start()
-
-    def from_north():
-        last_row.wait_recv()
-        last_cell.wait_recv()
-        for h in range(halves):
-            grid[h, 0, 7:8, :] = corner[h, 7:8, :]
-
-    def no_north():
-        grid[:, 0] = jnp.zeros((halves,) + grid.shape[2:], grid.dtype)
 
     for h in range(halves):
         grid[h, :, 0:8, :] = jnp.zeros((2 * rows + 1, 8, LANES), grid.dtype)
@@ -158,7 +135,7 @@
         seas = [mask[STEP * p + r][:, :chans] for r in range(STEP)]
         masked = [line * sea for line, sea in zip(lines, seas)]
         for q in range(1, sectors):
-            down[1 + p, 1 + q] = gather(masked, q).astype(down.dtype)
+            down[3 + p, 3 + q] = gather(masked, q).astype(down.dtype)
         return gather(lines, 0), gather(seas, 0)
 
     def later_band(p, carry):
@@ -167,7 +144,35 @@
         open_sea[p] = sea
         return carry
 
+    def halo(k, dp, dq, p, count, q, wide):
+        src = down.at[3 + p : 3 + p + count, 3 + q : 3 + q + wide]
+        to_p, to_q = 3 + p - dp * bands, 3 + q - dq * sectors
+        dst = down.at[to_p : to_p + count, to_q : to_q + wide]
+        return dp, remote(src, dst, down_sem, k, dp, dq)
+
+    far = bands - 3
+    east = [halo(0, 0, 1, far, 3, sectors - 3, 3), halo(1, 0, 1, 1, far - 1, sectors - 3, 3)]
+    west_side = [halo(2, 0, -1, far, 3, 0, 3), halo(3, 0, -1, 1, far - 1, 0, 3)]
+    south = [halo(4, 1, 0, far, 3, 0, sectors)]
+    top = [halo(5, 0, 1, 0, 1, sectors - 3, 3), halo(6, 0, -1, 0, 1, 0, 3)]
+    north = [halo(7, -1, 0, 0, 3, 0, sectors), halo(8, -1, 1, 0, 3, sectors - 3, 3),
+             halo(9, -1, -1, 0, 3, 0, 3)]
+
+    def forward(k, q):
+        return 1, remote(down.at[3 + far : 6 + far, q : q + 3], down.at[0:3, q : q + 3], down_sem, k, 1, 0)
+
+    corners = [forward(10, 0), forward(11, 3 + sectors)]
+
+    def start(copies):
+        for dp, copy in copies:
+            when(dp, copy.start)
+
+    def arrive(copies):
+        for dp, copy in copies:
+            when(-dp, copy.wait_recv)
+
     lax.fori_loop(1, bands, later_band, 0)
+    start(east)
 
     last_col.wait_recv()
     for h in range(halves):
@@ -179,7 +184,9 @@
     for p in range(1, bands):
         extra = jnp.concatenate(
             [late[h, STEP * STEP * p : STEP * STEP * (p + 1), :] for h in range(halves)], axis=1)
-        down[1 + p, 1] = ((open_block[p] + extra) * open_sea[p]).astype(down.dtype)
+        down[3 + p, 3] = ((open_block[p] + extra) * open_sea[p]).astype(down.dtype)
+
+    start(west_side + south)
 
     def from_north():
         last_row.wait_recv()
@@ -192,48 +199,14 @@
             grid[h, 1 + r, 7:8, :] = west[h, r : r + 1, :]
     pl.when(has[-1])(from_north)
     block, sea = down_band(0)
-    down[1, 1] = (block * sea).astype(down.dtype)
-
-    def exchange(buffer, width, sems):
-        def part(d, count, target):
-            if d == 0:
-                return slice(width, width + count)
-            if (d > 0) != target:
-                return slice(count, count + width) if d > 0 else slice(count + width, count + 2 * width)
-            return slice(0, width) if target else slice(width, 2 * width)
-
-        copies = []
-        for k, (dp, dq) in enumerate(SIDES):
-            src = buffer.at[part(dp, bands, False), part(dq, sectors, False)]
-            dst = buffer.at[part(dp, bands, True), part(dq, sectors, True)]
-            copies.append((dp, remote(src, dst, sems, k, dp, dq)))
-        return copies
-
-    def start(copies):
-        for dp, copy in copies:
-            when(dp, copy.start)
-
-    def arrive(copies):
-        for dp, copy in copies:
-            when(-dp, copy.wait_recv)
-
-    moves = exchange(down, 1, down_sem)
-    start(moves)
-    load_one.wait()
-    load_two.wait()
-    if tail:
-        for t in range(9):
-            two_tail[t] = jnp.zeros(two_tail.shape[1:], two_tail.dtype)
-            two_tail[t, 0:tail, :] = two[t // 3, t % 3, main:feats, :]
-    arrive(moves)
-
-    chunk = bands // 2
-    flat = chunk * sectors * STEP * STEP
-
-    def first(c, carry):
-        p = c * chunk
+    down[3, 3] = (block * sea).astype(down.dtype)
+
+    start(top + north)
+
+    def first(p, count, q, wide):
+        flat = count * wide * STEP * STEP
         pieces = [
-            down[pl.ds(p + a, chunk), b : b + sectors].reshape(flat, chans)
+            down[p + a : p + a + count, q + b : q + b + wide].reshape(flat, chans)
             for a in range(3) for b in range(3)
         ]
         total = lax.dot_general(
@@ -241,35 +214,32 @@
             jnp.concatenate([one[a, b] for a in range(3) for b in range(3)], axis=1),
             (((1,), (1,)), ((), ())), preferred_element_type=jnp.float32)
         value = gelu(total + b_one[...].reshape(1, feats)).astype(hidden.dtype)
-        hidden[pl.ds(2 + p, chunk), 2 : 2 + sectors, :, 0:feats] = value.reshape(
-            chunk, sectors, STEP * STEP, feats)
-        return carry
-
-    lax.fori_loop(0, 2, first, 0)
-
-    def side(k, dq, first, count):
-        buffer, q = (from_w, 2 + sectors - 2) if dq > 0 else (from_e, 2)
-        return remote(hidden.at[2 + first : 2 + first + count, q : q + 2],
-                      buffer.at[2 + first : 2 + first + count], hidden_sem, k, 0, dq)
-
-    outer = [side(0, 1, 0, 2), side(1, -1, 0, 2), side(2, 1, bands - 2, 2), side(3, -1, bands - 2, 2)]
-    inner = [side(4, 1, 2, bands - 4), side(5, -1, 2, bands - 4)]
-    own = slice(2, 2 + sectors)
-    lat_moves = [
-        (-1, remote(hidden.at[2:4, own], from_s.at[:, own], hidden_sem, 6, -1, 0)),
-        (1, remote(hidden.at[bands : bands + 2, own], from_n.at[:, own], hidden_sem, 7, 1, 0)),
-    ]
-    corners = [
-        (-1, remote(from_w.at[2:4], from_w.at[bands + 2 :], hidden_sem, 8, -1, 0)),
-        (-1, remote(from_e.at[2:4], from_e.at[bands + 2 :], hidden_sem, 9, -1, 0)),
-        (1, remote(from_w.at[bands : bands + 2], from_w.at[0:2], hidden_sem, 10, 1, 0)),
-        (1, remote(from_e.at[bands : bands + 2], from_e.at[0:2], hidden_sem, 11, 1, 0)),
-    ]
-    for copy in outer:
-        copy.start()
-    start(lat_moves)
-    for copy in inner:
-        copy.start()
+        hidden[p : p + count, q : q + wide, :, 0:feats] = value.reshape(
+            count, wide, STEP * STEP, feats)
+
+    load_one.wait()
+    first(3, bands - 2, 3, sectors - 2)
+    arrive(east[:1] + west_side[:1])
+    start(corners)
+    load_two.wait()
+    if tail:
+        for t in range(9):
+            two_tail[t] = jnp.zeros(two_tail.shape[1:], two_tail.dtype)
+            two_tail[t, 0:tail, :] = two[t // 3, t % 3, main:feats, :]
+    arrive(east[1:] + top[:1])
+    first(3, bands - 2, 0, 3)
+    arrive(west_side[1:] + top[1:])
+    first(3, bands - 2, sectors + 1, 3)
+    arrive(south + corners)
+    first(0, 3, 0, sectors + 4)
+
+    def no_cells(lat_at, p):
+        def body():
+            hidden[p : p + 2] = jnp.zeros((2,) + hidden.shape[1:], hidden.dtype)
+
+        pl.when(lat == lat_at)(body)
+
+    no_cells(0, 0)
 
     def taps_of(buffer, places, taps, size):
         count = size[0] * size[1] * STEP * STEP
@@ -289,6 +259,7 @@
         return total.reshape(size + (STEP * STEP, feats))
 
     every = [(a, b) for a in range(3) for b in range(3)]
+    chunk = bands // 2
 
     def second(c):
         p = c * chunk
@@ -296,20 +267,10 @@
             hidden, [(p + 2 * a, 2 * b) for a, b in every], every, (chunk, sectors))
 
     second(0)
-    for copy in outer:
-        copy.wait_recv()
-    start(corners)
+    arrive(north)
+    first(bands + 1, 3, 0, sectors + 4)
+    no_cells(n_lat - 1, bands + 2)
     second(1)
-    arrive(lat_moves)
-    sums[0:2] += taps_of(from_n, [(0, 2 * b) for b in range(3)], [(0, b) for b in range(3)], (2, sectors))
-    sums[bands - 2 :] += taps_of(
-        from_s, [(0, 2 * b) for b in range(3)], [(2, b) for b in range(3)], (2, sectors))
-    for copy in inner:
-        copy.wait_recv()
-    arrive(corners)
-    sums[:, 0:2] += taps_of(from_w, [(2 * a, 0) for a in range(3)], [(a, 0) for a in range(3)], (bands, 2))
-    sums[:, sectors - 2 :] += taps_of(
-        from_e, [(2 * a, 0) for a in range(3)], [(a, 2) for a in range(3)], (bands, 2))
 
     def finish(p, carry):
         value = gelu(sums[p] + b_two[...].reshape(1, 1, feats))
@@ -321,16 +282,8 @@
     lax.fori_loop(0, bands, finish, 0)
 
     last_col.wait_send()
-
-    def sent_south():
-        last_row.wait_send()
-        last_cell.wait_send()
-
-    when(1, sent_south)
-    for dp, copy in moves + lat_moves + corners:
+    for dp, copy in [(1, last_row), (1, last_cell)] + east + west_side + south + top + north + corners:
         when(dp, copy.wait_send)
-    for copy in outer + inner:
-        copy.wait_send()
 
 
 def on_device(n_lat, n_lon, fields, land_sea, w_depth, b_depth, w_one, b_one, w_two, b_two):
@@ -357,19 +310,14 @@
             pltpu.VMEM((bands, STEP * STEP, chans), jnp.float32),
             pltpu.VMEM((bands, STEP * STEP, chans), jnp.float32),
             pltpu.VMEM((rows, cols, wide), jnp.float32),
-            pltpu.VMEM((bands + 2, sectors + 2, STEP * STEP, chans), jnp.bfloat16),
+            pltpu.VMEM((bands + 6, sectors + 6, STEP * STEP, chans), jnp.bfloat16),
             pltpu.VMEM((bands + 4, sectors + 4, STEP * STEP, wide), jnp.bfloat16),
             pltpu.VMEM(taps_out_in.shape, jnp.bfloat16),
             pltpu.VMEM(w_two.shape, jnp.bfloat16),
             pltpu.VMEM((9, max(wide - main, LANES), feats), jnp.bfloat16),
-            pltpu.VMEM((2, sectors + 4, STEP * STEP, wide), jnp.bfloat16),
-            pltpu.VMEM((2, sectors + 4, STEP * STEP, wide), jnp.bfloat16),
-            pltpu.VMEM((bands + 4, 2, STEP * STEP, wide), jnp.bfloat16),
-            pltpu.VMEM((bands + 4, 2, STEP * STEP, wide), jnp.bfloat16),
             pltpu.VMEM((bands, sectors, STEP * STEP, feats), jnp.float32),
             pltpu.SemaphoreType.DMA((2 + 2 * halves,)),
             pltpu.SemaphoreType.DMA((2, 3)),
-            pltpu.SemaphoreType.DMA((2, len(SIDES))),
             pltpu.SemaphoreType.DMA((2, 12)),
         ],
         compiler_params=pltpu.CompilerParams(

time: 24.5 us -> 19.8 us (0.81)
  the two profiles are of different devices: /device:TPU:0 before, /device:TPU:19 now
where the time goes in v4:
time: 19.8 us; the launch traced here: 19.6 us
  Pallas kernels  18.7 us (94%)
  local copies, waits for them, and re-layouts  0.88 us (4%)
    pallas_call x1, Pallas kernels, on_device(): pl.pallas_call(functools.partial(kernel, (n_lat, n_lon, rows, cols, chans...  18.7 us
    unnamed x1, local copies, waits for them, and re-layouts  0.88 us

profile of v4, /device:TPU:19, one launch (start us, length us, event | category | flops | bytes accessed | tf_op | source)
XLA Modules:
  0.0 19.6 jit_solution(12461886752396332184)
XLA Ops:
  0.0 18.7 %shard_map.82 = f32[32,16,300]{2,1,0:T(8,128)S(1)} custom-call(f32[64,32,256]{2,1,0:T(8,128)} %fields.1, s32[16,32]{1,0:T(8,128)} %bitcast.3, f32[3,3,256]{2,1,0:T(4,128)} %w_depth.1, f32[256]{0:T(256)} %b_depth.1, bf16[3,3,300,256]{3,2,1,0:T(8,128)(2,1)} %bitcast.2, f32[300]{0:T(512)} %b_one.1, bf16[3,3,300,300]{3,2,1,0:T(8,128)(2,1)} %w_two.1, f32[300]{0:T(512)} %b_two.1), custom_call_target="tpu_custom_call" | custom-call | tf_op jit(solution)/shard_map/pallas_call | solution.py:299
  18.7 0.9 %copy.10 = f32[32,16,300]{2,1,0:T(8,128)} copy(f32[32,16,300]{2,1,0:T(8,128)S(1)} %shard_map.82) | data formatting | bytes 1228800

commit v5 on v4

--- a/solution.py
+++ b/solution.py
@@ -23,7 +23,7 @@
 
 def kernel(
     shape, fields, land, w_depth, b_depth, w_one, b_one, w_two, b_two, out,
-    grid, edge, west, corner, late, open_block, open_sea, mask, down, hidden, one, two, two_tail, sums,
+    grid, edge, west, corner, late, open_block, open_sea, mask, down, hidden, one, one_in_out, two, two_tail, sums,
     load_sem, edge_sem, down_sem,
 ):
     n_lat, n_lon, rows, cols, chans, feats = shape
@@ -150,18 +150,24 @@
         dst = down.at[to_p : to_p + count, to_q : to_q + wide]
         return dp, remote(src, dst, down_sem, k, dp, dq)
 
-    far = bands - 3
-    east = [halo(0, 0, 1, far, 3, sectors - 3, 3), halo(1, 0, 1, 1, far - 1, sectors - 3, 3)]
-    west_side = [halo(2, 0, -1, far, 3, 0, 3), halo(3, 0, -1, 1, far - 1, 0, 3)]
-    south = [halo(4, 1, 0, far, 3, 0, sectors)]
-    top = [halo(5, 0, 1, 0, 1, sectors - 3, 3), halo(6, 0, -1, 0, 1, 0, 3)]
-    north = [halo(7, -1, 0, 0, 3, 0, sectors), halo(8, -1, 1, 0, 3, sectors - 3, 3),
-             halo(9, -1, -1, 0, 3, 0, 3)]
-
-    def forward(k, q):
-        return 1, remote(down.at[3 + far : 6 + far, q : q + 3], down.at[0:3, q : q + 3], down_sem, k, 1, 0)
-
-    corners = [forward(10, 0), forward(11, 3 + sectors)]
+    far, last = bands - 3, sectors - 3
+    east = [halo(0, 0, 1, far, 3, last, 3), halo(1, 0, 1, 1, far - 1, last, 3)]
+    west_side = [halo(2, 0, -1, far, 3, 1, 2), halo(3, 0, -1, 1, far - 1, 1, 2)]
+    south = [halo(4, 1, 0, far, 3, 1, sectors - 1)]
+    north = [halo(5, -1, 0, 1, 2, 1, sectors - 1), halo(6, -1, 1, 1, 2, last, 3),
+             halo(7, -1, -1, 1, 2, 1, 2)]
+    west_late = [halo(8, 0, -1, far, 3, 0, 1), halo(9, 0, -1, 0, far, 0, 1)]
+    south_late = [halo(10, 1, 0, far, 3, 0, 1)]
+    top = [halo(11, 0, 1, 0, 1, last, 3), halo(12, 0, -1, 0, 1, 1, 2)]
+    north_late = [halo(13, -1, 0, 0, 1, 0, sectors), halo(14, -1, 0, 1, 2, 0, 1),
+                  halo(15, -1, 1, 0, 1, last, 3),
+                  halo(16, -1, -1, 0, 1, 0, 3), halo(17, -1, -1, 1, 2, 0, 1)]
+
+    def forward(k, q, wide):
+        return 1, remote(
+            down.at[3 + far : 6 + far, q : q + wide], down.at[0:3, q : q + wide], down_sem, k, 1, 0)
+
+    corners = [forward(18, 0, 3), forward(19, 4 + sectors, 2), forward(20, 3 + sectors, 1)]
 
     def start(copies):
         for dp, copy in copies:
@@ -172,7 +178,7 @@
             when(-dp, copy.wait_recv)
 
     lax.fori_loop(1, bands, later_band, 0)
-    start(east)
+    start(east[:1] + west_side[:1] + north[1:] + east[1:] + west_side[1:] + south + north[:1])
 
     last_col.wait_recv()
     for h in range(halves):
@@ -186,8 +192,6 @@
             [late[h, STEP * STEP * p : STEP * STEP * (p + 1), :] for h in range(halves)], axis=1)
         down[3 + p, 3] = ((open_block[p] + extra) * open_sea[p]).astype(down.dtype)
 
-    start(west_side + south)
-
     def from_north():
         last_row.wait_recv()
         last_cell.wait_recv()
@@ -201,7 +205,7 @@
     block, sea = down_band(0)
     down[3, 3] = (block * sea).astype(down.dtype)
 
-    start(top + north)
+    start(west_late + north_late[2:] + top + south_late + north_late[:2])
 
     def first(p, count, q, wide):
         flat = count * wide * STEP * STEP
@@ -209,18 +213,30 @@
             down[p + a : p + a + count, q + b : q + b + wide].reshape(flat, chans)
             for a in range(3) for b in range(3)
         ]
-        total = lax.dot_general(
-            jnp.concatenate(pieces, axis=1),
-            jnp.concatenate([one[a, b] for a in range(3) for b in range(3)], axis=1),
-            (((1,), (1,)), ((), ())), preferred_element_type=jnp.float32)
+        total = jnp.dot(
+            jnp.concatenate(pieces, axis=1), one_in_out[...].reshape(9 * chans, feats),
+            preferred_element_type=jnp.float32)
         value = gelu(total + b_one[...].reshape(1, feats)).astype(hidden.dtype)
         hidden[p : p + count, q : q + wide, :, 0:feats] = value.reshape(
             count, wide, STEP * STEP, feats)
 
     load_one.wait()
+
+    def turn(t, carry):
+        tap = one.at[t // 3, lax.rem(t, 3)]
+        one_in_out[t, :, 0:main] = jnp.transpose(tap[0:main, :])
+        if tail:
+            rest = jnp.concatenate(
+                [tap[main:feats, :], jnp.zeros((up_to(tail, LANES) - tail, chans), one.dtype)], axis=0)
+            one_in_out[t, :, main:feats] = jnp.transpose(rest)[:, 0:tail]
+        return carry
+
+    lax.fori_loop(0, 9, turn, 0)
+    arrive(east[:1] + west_side[:1])
+    start(corners[:2])
     first(3, bands - 2, 3, sectors - 2)
-    arrive(east[:1] + west_side[:1])
-    start(corners)
+    arrive(west_late[:1])
+    start(corners[2:])
     load_two.wait()
     if tail:
         for t in range(9):
@@ -228,9 +244,9 @@
             two_tail[t, 0:tail, :] = two[t // 3, t % 3, main:feats, :]
     arrive(east[1:] + top[:1])
     first(3, bands - 2, 0, 3)
-    arrive(west_side[1:] + top[1:])
+    arrive(west_side[1:] + west_late[1:] + top[1:])
     first(3, bands - 2, sectors + 1, 3)
-    arrive(south + corners)
+    arrive(south + south_late + corners)
     first(0, 3, 0, sectors + 4)
 
     def no_cells(lat_at, p):
@@ -267,7 +283,7 @@
             hidden, [(p + 2 * a, 2 * b) for a, b in every], every, (chunk, sectors))
 
     second(0)
-    arrive(north)
+    arrive(north + north_late)
     first(bands + 1, 3, 0, sectors + 4)
     no_cells(n_lat - 1, bands + 2)
     second(1)
@@ -282,7 +298,8 @@
     lax.fori_loop(0, bands, finish, 0)
 
     last_col.wait_send()
-    for dp, copy in [(1, last_row), (1, last_cell)] + east + west_side + south + top + north + corners:
+    for dp, copy in [(1, last_row), (1, last_cell)] + (
+            east + west_side + south + north + west_late + south_late + top + north_late + corners):
         when(dp, copy.wait_send)
 
 
@@ -313,12 +330,13 @@
             pltpu.VMEM((bands + 6, sectors + 6, STEP * STEP, chans), jnp.bfloat16),
             pltpu.VMEM((bands + 4, sectors + 4, STEP * STEP, wide), jnp.bfloat16),
             pltpu.VMEM(taps_out_in.shape, jnp.bfloat16),
+            pltpu.VMEM((9, chans, feats), jnp.bfloat16),
             pltpu.VMEM(w_two.shape, jnp.bfloat16),
             pltpu.VMEM((9, max(wide - main, LANES), feats), jnp.bfloat16),
             pltpu.VMEM((bands, sectors, STEP * STEP, feats), jnp.float32),
             pltpu.SemaphoreType.DMA((2 + 2 * halves,)),
             pltpu.SemaphoreType.DMA((2, 3)),
-            pltpu.SemaphoreType.DMA((2, 12)),
+            pltpu.SemaphoreType.DMA((2, 21)),
         ],
         compiler_params=pltpu.CompilerParams(
             collective_id=0, has_side_effects=True, vmem_limit_bytes=62 * 1024 * 1024),

time: 19.8 us -> 21.2 us (1.071)
  the two profiles are of different devices: /device:TPU:19 before, /device:TPU:0 now
where the time goes in v5:
time: 21.2 us; the launch traced here: 21 us
  Pallas kernels  20.1 us (95%)
  local copies, waits for them, and re-layouts  0.88 us (4%)
    pallas_call x1, Pallas kernels, on_device(): pl.pallas_call(functools.partial(kernel, (n_lat, n_lon, rows, cols, chans...  20.1 us
    unnamed x1, local copies, waits for them, and re-layouts  0.88 us

profile of v5, /device:TPU:0, one launch (start us, length us, event | category | flops | bytes accessed | tf_op | source)
XLA Modules:
  0.0 21.0 jit_solution(1647400530757108663)
XLA Ops:
  0.0 20.1 %shard_map.82 = f32[32,16,300]{2,1,0:T(8,128)S(1)} custom-call(f32[64,32,256]{2,1,0:T(8,128)} %fields.1, s32[16,32]{1,0:T(8,128)} %bitcast.3, f32[3,3,256]{2,1,0:T(4,128)} %w_depth.1, f32[256]{0:T(256)} %b_depth.1, bf16[3,3,300,256]{3,2,1,0:T(8,128)(2,1)} %bitcast.2, f32[300]{0:T(512)} %b_one.1, bf16[3,3,300,300]{3,2,1,0:T(8,128)(2,1)} %w_two.1, f32[300]{0:T(512)} %b_two.1), custom_call_target="tpu_custom_call" | custom-call | tf_op jit(solution)/shard_map/pallas_call | solution.py:316
  20.1 0.9 %copy.10 = f32[32,16,300]{2,1,0:T(8,128)} copy(f32[32,16,300]{2,1,0:T(8,128)S(1)} %shard_map.82) | data formatting | bytes 1228800

commit v6 on v5

--- a/solution.py
+++ b/solution.py
@@ -23,7 +23,7 @@
 
 def kernel(
     shape, fields, land, w_depth, b_depth, w_one, b_one, w_two, b_two, out,
-    grid, edge, west, corner, late, open_block, open_sea, mask, down, hidden, one, one_in_out, two, two_tail, sums,
+    grid, edge, west, corner, late, open_block, open_sea, mask, down, hidden, one, two, two_tail, sums,
     load_sem, edge_sem, down_sem,
 ):
     n_lat, n_lon, rows, cols, chans, feats = shape
@@ -67,8 +67,9 @@
     for i in range(rows):
         mask[i] = jnp.broadcast_to(cells[:, i : i + 1], mask.shape[1:])
 
-    for p in range(bands + 4):
-        hidden[p] = jnp.zeros(hidden.shape[1:], hidden.dtype)
+    if tail:
+        for p in range(bands + 4):
+            hidden[p, :, :, main:] = jnp.zeros(hidden.shape[1:3] + (hidden.shape[3] - main,), hidden.dtype)
 
     def clear(buffer, width):
         gap = jnp.zeros((width,) + buffer.shape[1:], buffer.dtype)
@@ -167,7 +168,7 @@
         return 1, remote(
             down.at[3 + far : 6 + far, q : q + wide], down.at[0:3, q : q + wide], down_sem, k, 1, 0)
 
-    corners = [forward(18, 0, 3), forward(19, 4 + sectors, 2), forward(20, 3 + sectors, 1)]
+    corners = [forward(18, 0, 3), forward(19, 3 + sectors, 3)]
 
     def start(copies):
         for dp, copy in copies:
@@ -213,30 +214,18 @@
             down[p + a : p + a + count, q + b : q + b + wide].reshape(flat, chans)
             for a in range(3) for b in range(3)
         ]
-        total = jnp.dot(
-            jnp.concatenate(pieces, axis=1), one_in_out[...].reshape(9 * chans, feats),
-            preferred_element_type=jnp.float32)
+        total = lax.dot_general(
+            jnp.concatenate(pieces, axis=1),
+            jnp.concatenate([one[a, b] for a in range(3) for b in range(3)], axis=1),
+            (((1,), (1,)), ((), ())), preferred_element_type=jnp.float32)
         value = gelu(total + b_one[...].reshape(1, feats)).astype(hidden.dtype)
         hidden[p : p + count, q : q + wide, :, 0:feats] = value.reshape(
             count, wide, STEP * STEP, feats)
 
     load_one.wait()
-
-    def turn(t, carry):
-        tap = one.at[t // 3, lax.rem(t, 3)]
-        one_in_out[t, :, 0:main] = jnp.transpose(tap[0:main, :])
-        if tail:
-            rest = jnp.concatenate(
-                [tap[main:feats, :], jnp.zeros((up_to(tail, LANES) - tail, chans), one.dtype)], axis=0)
-            one_in_out[t, :, main:feats] = jnp.transpose(rest)[:, 0:tail]
-        return carry
-
-    lax.fori_loop(0, 9, turn, 0)
-    arrive(east[:1] + west_side[:1])
-    start(corners[:2])
     first(3, bands - 2, 3, sectors - 2)
-    arrive(west_late[:1])
-    start(corners[2:])
+    arrive(east[:1] + west_side[:1] + west_late[:1])
+    start(corners)
     load_two.wait()
     if tail:
         for t in range(9):
@@ -330,13 +319,12 @@
             pltpu.VMEM((bands + 6, sectors + 6, STEP * STEP, chans), jnp.bfloat16),
             pltpu.VMEM((bands + 4, sectors + 4, STEP * STEP, wide), jnp.bfloat16),
             pltpu.VMEM(taps_out_in.shape, jnp.bfloat16),
-            pltpu.VMEM((9, chans, feats), jnp.bfloat16),
             pltpu.VMEM(w_two.shape, jnp.bfloat16),
             pltpu.VMEM((9, max(wide - main, LANES), feats), jnp.bfloat16),
             pltpu.VMEM((bands, sectors, STEP * STEP, feats), jnp.float32),
             pltpu.SemaphoreType.DMA((2 + 2 * halves,)),
             pltpu.SemaphoreType.DMA((2, 3)),
-            pltpu.SemaphoreType.DMA((2, 21)),
+            pltpu.SemaphoreType.DMA((2, 20)),
         ],
         compiler_params=pltpu.CompilerParams(
             collective_id=0, has_side_effects=True, vmem_limit_bytes=62 * 1024 * 1024),

time: 21.2 us -> 21.4 us (level)
  no operation moved by 1% of the time
where the time goes in v6:
time: 21.4 us; the launch traced here: 21 us
  Pallas kernels  20.1 us (94%)
  local copies, waits for them, and re-layouts  0.88 us (4%)
    pallas_call x1, Pallas kernels, on_device(): pl.pallas_call(functools.partial(kernel, (n_lat, n_lon, rows, cols, chans...  20.1 us
    unnamed x1, local copies, waits for them, and re-layouts  0.88 us

profile of v6, /device:TPU:0, one launch (start us, length us, event | category | flops | bytes accessed | tf_op | source)
XLA Modules:
  0.0 21.0 jit_solution(5423367388385568322)
XLA Ops:
  0.0 20.1 %shard_map.82 = f32[32,16,300]{2,1,0:T(8,128)S(1)} custom-call(f32[64,32,256]{2,1,0:T(8,128)} %fields.1, s32[16,32]{1,0:T(8,128)} %bitcast.3, f32[3,3,256]{2,1,0:T(4,128)} %w_depth.1, f32[256]{0:T(256)} %b_depth.1, bf16[3,3,300,256]{3,2,1,0:T(8,128)(2,1)} %bitcast.2, f32[300]{0:T(512)} %b_one.1, bf16[3,3,300,300]{3,2,1,0:T(8,128)(2,1)} %w_two.1, f32[300]{0:T(512)} %b_two.1), custom_call_target="tpu_custom_call" | custom-call | tf_op jit(solution)/shard_map/pallas_call | solution.py:305
  20.1 0.9 %copy.10 = f32[32,16,300]{2,1,0:T(8,128)} copy(f32[32,16,300]{2,1,0:T(8,128)S(1)} %shard_map.82) | data formatting | bytes 1228800

commit v7 on v4

--- a/solution.py
+++ b/solution.py
@@ -23,7 +23,7 @@
 
 def kernel(
     shape, fields, land, w_depth, b_depth, w_one, b_one, w_two, b_two, out,
-    grid, edge, west, corner, late, open_block, open_sea, mask, down, hidden, one, two, two_tail, sums,
+    grid, edge, west, corner, late, open_block, open_sea, mask, down, hidden, one, one_in_out, two, two_tail, sums,
     load_sem, edge_sem, down_sem,
 ):
     n_lat, n_lon, rows, cols, chans, feats = shape
@@ -67,8 +67,9 @@
     for i in range(rows):
         mask[i] = jnp.broadcast_to(cells[:, i : i + 1], mask.shape[1:])
 
-    for p in range(bands + 4):
-        hidden[p] = jnp.zeros(hidden.shape[1:], hidden.dtype)
+    if tail:
+        for p in range(bands + 4):
+            hidden[p, :, :, main:] = jnp.zeros(hidden.shape[1:3] + (hidden.shape[3] - main,), hidden.dtype)
 
     def clear(buffer, width):
         gap = jnp.zeros((width,) + buffer.shape[1:], buffer.dtype)
@@ -209,15 +210,25 @@
             down[p + a : p + a + count, q + b : q + b + wide].reshape(flat, chans)
             for a in range(3) for b in range(3)
         ]
-        total = lax.dot_general(
-            jnp.concatenate(pieces, axis=1),
-            jnp.concatenate([one[a, b] for a in range(3) for b in range(3)], axis=1),
-            (((1,), (1,)), ((), ())), preferred_element_type=jnp.float32)
+        total = jnp.dot(
+            jnp.concatenate(pieces, axis=1), one_in_out[...].reshape(9 * chans, feats),
+            preferred_element_type=jnp.float32)
         value = gelu(total + b_one[...].reshape(1, feats)).astype(hidden.dtype)
         hidden[p : p + count, q : q + wide, :, 0:feats] = value.reshape(
             count, wide, STEP * STEP, feats)
 
     load_one.wait()
+
+    def turn(t, carry):
+        tap = one.at[t // 3, lax.rem(t, 3)]
+        one_in_out[t, :, 0:main] = jnp.transpose(tap[0:main, :])
+        if tail:
+            rest = jnp.concatenate(
+                [tap[main:feats, :], jnp.zeros((up_to(tail, LANES) - tail, chans), one.dtype)], axis=0)
+            one_in_out[t, :, main:feats] = jnp.transpose(rest)[:, 0:tail]
+        return carry
+
+    lax.fori_loop(0, 9, turn, 0)
     first(3, bands - 2, 3, sectors - 2)
     arrive(east[:1] + west_side[:1])
     start(corners)
@@ -259,18 +270,11 @@
         return total.reshape(size + (STEP * STEP, feats))
 
     every = [(a, b) for a in range(3) for b in range(3)]
-    chunk = bands // 2
-
-    def second(c):
-        p = c * chunk
-        sums[p : p + chunk] = taps_of(
-            hidden, [(p + 2 * a, 2 * b) for a, b in every], every, (chunk, sectors))
-
-    second(0)
-    arrive(north)
-    first(bands + 1, 3, 0, sectors + 4)
-    no_cells(n_lat - 1, bands + 2)
-    second(1)
+    early = bands - 3
+
+    def second(p, count):
+        sums[p : p + count] = taps_of(
+            hidden, [(p + 2 * a, 2 * b) for a, b in every], every, (count, sectors))
 
     def finish(p, carry):
         value = gelu(sums[p] + b_two[...].reshape(1, 1, feats))
@@ -279,7 +283,13 @@
             out[i] = gather([value[q, STEP * r : STEP * r + STEP] for q in range(sectors)], 0) * mask[i][:, :feats]
         return carry
 
-    lax.fori_loop(0, bands, finish, 0)
+    second(0, early)
+    lax.fori_loop(0, early, finish, 0)
+    arrive(north)
+    first(bands + 1, 3, 0, sectors + 4)
+    no_cells(n_lat - 1, bands + 2)
+    second(early, bands - early)
+    lax.fori_loop(early, bands, finish, 0)
 
     last_col.wait_send()
     for dp, copy in [(1, last_row), (1, last_cell)] + east + west_side + south + top + north + corners:
@@ -313,6 +323,7 @@
             pltpu.VMEM((bands + 6, sectors + 6, STEP * STEP, chans), jnp.bfloat16),
             pltpu.VMEM((bands + 4, sectors + 4, STEP * STEP, wide), jnp.bfloat16),
             pltpu.VMEM(taps_out_in.shape, jnp.bfloat16),
+            pltpu.VMEM((9, chans, feats), jnp.bfloat16),
             pltpu.VMEM(w_two.shape, jnp.bfloat16),
             pltpu.VMEM((9, max(wide - main, LANES), feats), jnp.bfloat16),
             pltpu.VMEM((bands, sectors, STEP * STEP, feats), jnp.float32),

time: 19.8 us -> 19.8 us (level)
  the two profiles are of different devices: /device:TPU:19 before, /device:TPU:11 now
where the time goes in v7:
time: 19.8 us; the launch traced here: 19.5 us
  Pallas kernels  18.6 us (94%)
  local copies, waits for them, and re-layouts  0.88 us (4%)
    pallas_call x1, Pallas kernels, on_device(): pl.pallas_call(functools.partial(kernel, (n_lat, n_lon, rows, cols, chans...  18.6 us
    unnamed x1, local copies, waits for them, and re-layouts  0.88 us

profile of v7, /device:TPU:11, one launch (start us, length us, event | category | flops | bytes accessed | tf_op | source)
XLA Modules:
  0.0 19.5 jit_solution(14700897757896611490)
XLA Ops:
  0.0 18.6 %shard_map.82 = f32[32,16,300]{2,1,0:T(8,128)S(1)} custom-call(f32[64,32,256]{2,1,0:T(8,128)} %fields.1, s32[16,32]{1,0:T(8,128)} %bitcast.3, f32[3,3,256]{2,1,0:T(4,128)} %w_depth.1, f32[256]{0:T(256)} %b_depth.1, bf16[3,3,300,256]{3,2,1,0:T(8,128)(2,1)} %bitcast.2, f32[300]{0:T(512)} %b_one.1, bf16[3,3,300,300]{3,2,1,0:T(8,128)(2,1)} %w_two.1, f32[300]{0:T(512)} %b_two.1), custom_call_target="tpu_custom_call" | custom-call | tf_op jit(solution)/shard_map/pallas_call | solution.py:309
  18.7 0.9 %copy.10 = f32[32,16,300]{2,1,0:T(8,128)} copy(f32[32,16,300]{2,1,0:T(8,128)S(1)} %shard_map.82) | data formatting | bytes 1228800

commit v8 on v7

--- a/solution.py
+++ b/solution.py
@@ -156,13 +156,15 @@
     west_side = [halo(2, 0, -1, far, 3, 0, 3), halo(3, 0, -1, 1, far - 1, 0, 3)]
     south = [halo(4, 1, 0, far, 3, 0, sectors)]
     top = [halo(5, 0, 1, 0, 1, sectors - 3, 3), halo(6, 0, -1, 0, 1, 0, 3)]
-    north = [halo(7, -1, 0, 0, 3, 0, sectors), halo(8, -1, 1, 0, 3, sectors - 3, 3),
-             halo(9, -1, -1, 0, 3, 0, 3)]
-
-    def forward(k, q):
-        return 1, remote(down.at[3 + far : 6 + far, q : q + 3], down.at[0:3, q : q + 3], down_sem, k, 1, 0)
-
-    corners = [forward(10, 0), forward(11, 3 + sectors)]
+    north = [halo(7, -1, 0, 0, 3, 0, sectors)]
+
+    def forward(k, dp, q):
+        p, to_p = (3 + far, 0) if dp > 0 else (3, 3 + bands)
+        return dp, remote(
+            down.at[p : p + 3, q : q + 3], down.at[to_p : to_p + 3, q : q + 3], down_sem, k, dp, 0)
+
+    lower = [forward(8, 1, 0), forward(9, 1, 3 + sectors)]
+    upper = [forward(10, -1, 0), forward(11, -1, 3 + sectors)]
 
     def start(copies):
         for dp, copy in copies:
@@ -231,17 +233,19 @@
     lax.fori_loop(0, 9, turn, 0)
     first(3, bands - 2, 3, sectors - 2)
     arrive(east[:1] + west_side[:1])
-    start(corners)
+    start(lower)
     load_two.wait()
     if tail:
         for t in range(9):
             two_tail[t] = jnp.zeros(two_tail.shape[1:], two_tail.dtype)
             two_tail[t, 0:tail, :] = two[t // 3, t % 3, main:feats, :]
     arrive(east[1:] + top[:1])
+    start(upper[:1])
     first(3, bands - 2, 0, 3)
     arrive(west_side[1:] + top[1:])
+    start(upper[1:])
     first(3, bands - 2, sectors + 1, 3)
-    arrive(south + corners)
+    arrive(south + lower)
     first(0, 3, 0, sectors + 4)
 
     def no_cells(lat_at, p):
@@ -285,14 +289,14 @@
 
     second(0, early)
     lax.fori_loop(0, early, finish, 0)
-    arrive(north)
+    arrive(north + upper)
     first(bands + 1, 3, 0, sectors + 4)
     no_cells(n_lat - 1, bands + 2)
     second(early, bands - early)
     lax.fori_loop(early, bands, finish, 0)
 
     last_col.wait_send()
-    for dp, copy in [(1, last_row), (1, last_cell)] + east + west_side + south + top + north + corners:
+    for dp, copy in [(1, last_row), (1, last_cell)] + east + west_side + south + top + north + lower + upper:
         when(dp, copy.wait_send)
 
 

time: 19.8 us -> 19.9 us (level)
  the two profiles are of different devices: /device:TPU:11 before, /device:TPU:17 now
where the time goes in v8:
time: 19.9 us; the launch traced here: 19.6 us
  Pallas kernels  18.7 us (94%)
  local copies, waits for them, and re-layouts  0.88 us (4%)
    pallas_call x1, Pallas kernels, on_device(): pl.pallas_call(functools.partial(kernel, (n_lat, n_lon, rows, cols, chans...  18.7 us
    unnamed x1, local copies, waits for them, and re-layouts  0.88 us

profile of v8, /device:TPU:17, one launch (start us, length us, event | category | flops | bytes accessed | tf_op | source)
XLA Modules:
  0.0 19.6 jit_solution(9856643868926999148)
XLA Ops:
  0.0 18.7 %shard_map.82 = f32[32,16,300]{2,1,0:T(8,128)S(1)} custom-call(f32[64,32,256]{2,1,0:T(8,128)} %fields.1, s32[16,32]{1,0:T(8,128)} %bitcast.3, f32[3,3,256]{2,1,0:T(4,128)} %w_depth.1, f32[256]{0:T(256)} %b_depth.1, bf16[3,3,300,256]{3,2,1,0:T(8,128)(2,1)} %bitcast.2, f32[300]{0:T(512)} %b_one.1, bf16[3,3,300,300]{3,2,1,0:T(8,128)(2,1)} %w_two.1, f32[300]{0:T(512)} %b_two.1), custom_call_target="tpu_custom_call" | custom-call | tf_op jit(solution)/shard_map/pallas_call | solution.py:313
  18.8 0.9 %copy.10 = f32[32,16,300]{2,1,0:T(8,128)} copy(f32[32,16,300]{2,1,0:T(8,128)S(1)} %shard_map.82) | data formatting | bytes 1228800

commit v9 on v7

--- a/solution.py
+++ b/solution.py
@@ -23,7 +23,7 @@
 
 def kernel(
     shape, fields, land, w_depth, b_depth, w_one, b_one, w_two, b_two, out,
-    grid, edge, west, corner, late, open_block, open_sea, mask, down, hidden, one, one_in_out, two, two_tail, sums,
+    grid, edge, west, edge_sent, west_sent, corner, late, open_block, open_sea, mask, down, hidden, one, one_in_out, two, two_tail, sums,
     load_sem, edge_sem, down_sem,
 ):
     n_lat, n_lon, rows, cols, chans, feats = shape
@@ -93,6 +93,7 @@
         edge_parts[h].wait()
         for r in range(2 * rows):
             edge[h, r : r + 1, :] = grid[h, 1 + r, 8 + 2 * cols - 1 : 8 + 2 * cols, :]
+    edge_sent[...] = edge[...].astype(edge_sent.dtype)
 
     pl.semaphore_wait(barrier, 2 + 3 * jnp.minimum(lat, 1) + 3 * jnp.minimum(n_lat - 1 - lat, 1))
 
@@ -102,8 +103,8 @@
             device_id=device(dp, dq), device_id_type=MESH)
 
     last_row = remote(grid.at[:, 2 * rows, 8:, :], grid.at[:, 0, 8:, :], edge_sem, 0, 1, 0)
-    last_col = remote(edge, west, edge_sem, 1, 0, 1)
-    last_cell = remote(edge.at[:, 2 * rows - 8 :], corner, edge_sem, 2, 1, 1)
+    last_col = remote(edge_sent, west_sent, edge_sem, 1, 0, 1)
+    last_cell = remote(edge_sent.at[:, 2 * rows - 16 :], corner, edge_sem, 2, 1, 1)
     last_col.start()
     when(1, last_cell.start)
     for inner in inner_parts:
@@ -176,6 +177,7 @@
     start(east)
 
     last_col.wait_recv()
+    west[...] = west_sent[...].astype(west.dtype)
     for h in range(halves):
         lanes = slice(h * LANES, (h + 1) * LANES)
         from_west = sum(
@@ -193,7 +195,7 @@
         last_row.wait_recv()
         last_cell.wait_recv()
         for h in range(halves):
-            grid[h, 0, 7:8, :] = corner[h, 7:8, :]
+            grid[h, 0, 7:8, :] = corner[h].astype(grid.dtype)[15:16, :]
 
     for h in range(halves):
         for r in range(2 * STEP):
@@ -315,7 +317,9 @@
             pltpu.VMEM((halves, 2 * rows + 1, 2 * cols + 8, LANES), jnp.float32),
             pltpu.VMEM((halves, 2 * rows, LANES), jnp.float32),
             pltpu.VMEM((halves, 2 * rows, LANES), jnp.float32),
-            pltpu.VMEM((halves, 8, LANES), jnp.float32),
+            pltpu.VMEM((halves, 2 * rows, LANES), jnp.bfloat16),
+            pltpu.VMEM((halves, 2 * rows, LANES), jnp.bfloat16),
+            pltpu.VMEM((halves, 16, LANES), jnp.bfloat16),
             pltpu.VMEM((halves, STEP * rows, LANES), jnp.float32),
             pltpu.VMEM((bands, STEP * STEP, chans), jnp.float32),
             pltpu.VMEM((bands, STEP * STEP, chans), jnp.float32),

time: 19.8 us -> 19.3 us (0.975)
  the two profiles are of different devices: /device:TPU:11 before, /device:TPU:9 now
where the time goes in v9:
time: 19.3 us; the launch traced here: 19 us
  Pallas kernels  18.1 us (94%)
  local copies, waits for them, and re-layouts  0.88 us (5%)
    pallas_call x1, Pallas kernels, on_device(): pl.pallas_call(functools.partial(kernel, (n_lat, n_lon, rows, cols, chans...  18.1 us
    unnamed x1, local copies, waits for them, and re-layouts  0.88 us

profile of v9, /device:TPU:9, one launch (start us, length us, event | category | flops | bytes accessed | tf_op | source)
XLA Modules:
  0.0 19.0 jit_solution(5206225856689302330)
XLA Ops:
  0.0 18.1 %shard_map.82 = f32[32,16,300]{2,1,0:T(8,128)S(1)} custom-call(f32[64,32,256]{2,1,0:T(8,128)} %fields.1, s32[16,32]{1,0:T(8,128)} %bitcast.3, f32[3,3,256]{2,1,0:T(4,128)} %w_depth.1, f32[256]{0:T(256)} %b_depth.1, bf16[3,3,300,256]{3,2,1,0:T(8,128)(2,1)} %bitcast.2, f32[300]{0:T(512)} %b_one.1, bf16[3,3,300,300]{3,2,1,0:T(8,128)(2,1)} %w_two.1, f32[300]{0:T(512)} %b_two.1), custom_call_target="tpu_custom_call" | custom-call | tf_op jit(solution)/shard_map/pallas_call | solution.py:311
  18.1 0.9 %copy.10 = f32[32,16,300]{2,1,0:T(8,128)} copy(f32[32,16,300]{2,1,0:T(8,128)S(1)} %shard_map.82) | data formatting | bytes 1228800

commit v10 on v9

--- a/solution.py
+++ b/solution.py
@@ -204,7 +204,7 @@
     block, sea = down_band(0)
     down[3, 3] = (block * sea).astype(down.dtype)
 
-    start(top + north)
+    start(top[1:] + north[2:] + top[:1] + north[1:2] + north[:1])
 
     def first(p, count, q, wide):
         flat = count * wide * STEP * STEP

time: 19.3 us -> 19.8 us (1.026)
  the two profiles are of different devices: /device:TPU:9 before, /device:TPU:1 now
where the time goes in v10:
time: 19.8 us; the launch traced here: 19.6 us
  Pallas kernels  18.7 us (94%)
  local copies, waits for them, and re-layouts  0.88 us (4%)
    pallas_call x1, Pallas kernels, on_device(): pl.pallas_call(functools.partial(kernel, (n_lat, n_lon, rows, cols, chans...  18.7 us
    unnamed x1, local copies, waits for them, and re-layouts  0.88 us

profile of v10, /device:TPU:1, one launch (start us, length us, event | category | flops | bytes accessed | tf_op | source)
XLA Modules:
  0.0 19.6 jit_solution(16043801690743707746)
XLA Ops:
  0.0 18.7 %shard_map.82 = f32[32,16,300]{2,1,0:T(8,128)S(1)} custom-call(f32[64,32,256]{2,1,0:T(8,128)} %fields.1, s32[16,32]{1,0:T(8,128)} %bitcast.3, f32[3,3,256]{2,1,0:T(4,128)} %w_depth.1, f32[256]{0:T(256)} %b_depth.1, bf16[3,3,300,256]{3,2,1,0:T(8,128)(2,1)} %bitcast.2, f32[300]{0:T(512)} %b_one.1, bf16[3,3,300,300]{3,2,1,0:T(8,128)(2,1)} %w_two.1, f32[300]{0:T(512)} %b_two.1), custom_call_target="tpu_custom_call" | custom-call | tf_op jit(solution)/shard_map/pallas_call | solution.py:311
  18.7 0.9 %copy.10 = f32[32,16,300]{2,1,0:T(8,128)} copy(f32[32,16,300]{2,1,0:T(8,128)S(1)} %shard_map.82) | data formatting | bytes 1228800
